TPU v7x, 128 devices: a whole 4x4x4 slice. The times are simulated.
128 devices in a mesh: boxes: 32 (over x, y, core), grp: 4 (over z).
Axes of the slice: x: 4, y: 4, z: 4, core: 2. Of those that a mesh axis runs over, the one named last changes fastest.
Arguments:
- charges: bfloat16 [16, 4194304], P(None, ('boxes', 'grp')), may hold values from -6 to 6
- leaf_basis: bfloat16 [16384, 64, 256], P(('boxes', 'grp')), may hold values from -0.375 to 0.375
- transfer0: bfloat16 [16384, 4096], P(('boxes', 'grp')), may hold values from -0.375 to 0.375
- transfer1: bfloat16 [2048, 4096], P(('boxes', 'grp')), may hold values from -0.375 to 0.375
- transfer2: bfloat16 [256, 4096], P(('boxes', 'grp')), may hold values from -0.375 to 0.375
- coupling: bfloat16 [4, 316, 4096], replicated, may hold values from -0.0546875 to 0.0546875
- lists0: int32 [16384, 189], P(('boxes', 'grp')), may hold values from -1 to 16383, as said below
- lists1: int32 [2048, 189], P(('boxes', 'grp')), may hold values from -1 to 2047, as said below
- lists2: int32 [256, 189], P(('boxes', 'grp')), may hold values from -1 to 255, as said below
- lists3: int32 [32, 189], P('boxes'), may hold values from -1 to 31, as said below
- kinds0: int32 [16384, 189], P(('boxes', 'grp')), may hold values from 0 to 315
- kinds1: int32 [2048, 189], P(('boxes', 'grp')), may hold values from 0 to 315
- kinds2: int32 [256, 189], P(('boxes', 'grp')), may hold values from 0 to 315
- kinds3: int32 [32, 189], P('boxes'), may hold values from 0 to 315
Outputs:
- potential: bfloat16 [16, 4194304], P(None, ('boxes', 'grp'))
Inputs may be any that keep to these rules, and one draw needn't show every extreme that they name: `lists0`: each row names distinct leaf boxes by global Morton id, live entries first and -1 after them, at least one live. Device d owns leaf ids d * 128 to (d + 1) * 128 - 1, and its rows name boxes only of devices d - 13 to d + 13 and of the device half the devices away in Morton order; the lists of one device's leaf boxes name at most 32 distinct boxes of any one other device, and in every draw some pair of devices reaches 32. `lists1`: as for lists0, one level up: device d owns ids d * 16 onward, its rows name boxes only of devices d - 13 to d + 13 and of the device half the devices away, and at most 8 distinct boxes of one other device are named by one device's rows, reached in every draw. `lists2`: as for lists0, two levels up: device d owns ids d * 2 onward, its rows name boxes only of devices d - 13 to d + 13 and of the device half the devices away, and at most 2 distinct boxes of one other device are named by one device's rows, reached in every draw. `lists3`: each row names distinct boxes other than its own, live entries first and -1 after them, at least one live.
All inputs are finite; a program needn't handle non-finite values.
Results may differ from a plain program's by a relative error of at most 0.012.
Values may be sent and summed in bfloat16 or wider, within the bound.
A program may use at most 192 MiB of HBM per device.

v0:
```python
import jax
import jax.numpy as jnp
from jax import lax
from jax.sharding import PartitionSpec as P


def far_field(extended, places, slot_kinds, couple, rank_size, vector_count):
    rows_total, partners = places.shape
    kinds_count = couple.shape[0]
    block_rows = min(16, rows_total)
    couple_wide = couple.astype(jnp.float32).reshape(kinds_count, rank_size, rank_size)
    kind_range = jnp.arange(kinds_count, dtype=jnp.int32)

    def one_block(pair):
        chosen, which = pair
        sources = extended[chosen]
        selector = (which[..., None] == kind_range).astype(jnp.bfloat16)
        grouped = jnp.einsum("bpk,bpc->bkc", selector, sources, preferred_element_type=jnp.float32)
        grouped = grouped.reshape(block_rows, kinds_count, rank_size, vector_count)
        return jnp.einsum("krs,bksv->brv", couple_wide, grouped, precision=lax.Precision.HIGHEST)

    result = lax.map(
        one_block,
        (places.reshape(-1, block_rows, partners), slot_kinds.reshape(-1, block_rows, partners)),
    )
    return result.reshape(rows_total, rank_size * vector_count)


def request_plan(partner_ids, box_count, capacity, own_index, devices):
    owner_dev = partner_ids // box_count
    within = partner_ids % box_count
    remote = (partner_ids >= 0) & (owner_dev != own_index)
    owner_safe = jnp.clip(owner_dev, 0, devices - 1)
    flat_index = jnp.where(remote, owner_safe * box_count + within, devices * box_count).reshape(-1)
    needed = (
        jnp.zeros((devices * box_count + 1,), jnp.int32)
        .at[flat_index]
        .set(1)[:-1]
        .reshape(devices, box_count)
    )
    slot_rank = jnp.cumsum(needed, axis=1) - 1
    target = jnp.where(
        needed > 0,
        jnp.arange(devices, dtype=jnp.int32)[:, None] * capacity + slot_rank,
        devices * capacity,
    )
    fillers = jnp.tile(jnp.arange(box_count, dtype=jnp.int32), devices)
    requests = (
        jnp.full((devices * capacity + 1,), -1, jnp.int32)
        .at[target.reshape(-1)]
        .set(fillers)[:-1]
        .reshape(devices, capacity)
    )
    slot_index = slot_rank[owner_safe, within]
    places = jnp.where(
        remote,
        box_count + owner_safe * capacity + slot_index,
        jnp.where(partner_ids >= 0, within, box_count + devices * capacity),
    )
    return (requests, places)


def serve(asked, table):
    picked = table[jnp.maximum(asked, 0)]
    return jnp.where((asked >= 0)[..., None], picked, jnp.zeros_like(picked))


def extend(table, received):
    block_width = table.shape[1]
    return jnp.concatenate(
        [table, received.reshape(-1, block_width), jnp.zeros((1, block_width), table.dtype)], axis=0
    )


def whole_table(table, partner_ids):
    places = jnp.where(partner_ids >= 0, partner_ids, table.shape[0])
    padded = jnp.concatenate([table, jnp.zeros((1, table.shape[1]), table.dtype)], axis=0)
    return (padded, places)


def lift(transfer, children, rank_size, vector_count):
    matrices = transfer.reshape(-1, rank_size, rank_size)
    terms = jnp.einsum("bpc,bcv->bpv", matrices, children, preferred_element_type=jnp.float32)
    return jnp.sum(terms.reshape(-1, 8, rank_size, vector_count), axis=1)


def lower(transfer, parents, local_part, rank_size):
    matrices = transfer.reshape(-1, rank_size, rank_size)
    terms = jnp.einsum("bpc,bpv->bcv", matrices, parents, preferred_element_type=jnp.float32)
    return (local_part + terms.reshape(local_part.shape)).astype(jnp.bfloat16)


def on_device(
    charges,
    leaf_basis,
    transfer0,
    transfer1,
    transfer2,
    coupling,
    lists0,
    lists1,
    lists2,
    lists3,
    kinds0,
    kinds1,
    kinds2,
    kinds3,
):
    devices = lax.axis_size(("boxes", "grp"))
    own_index = lax.axis_index(("boxes", "grp"))
    member = lax.axis_index("grp")
    vector_count = charges.shape[0]
    leaf_boxes, rank_size, leaf_size = leaf_basis.shape
    mid_boxes = transfer1.shape[0]
    upper_boxes = transfer2.shape[0]
    block_width = rank_size * vector_count
    leaf_room = leaf_boxes // 4
    mid_room = leaf_boxes // 16
    upper_room = leaf_boxes // 64
    samples = charges.reshape(vector_count, leaf_boxes, leaf_size)
    leaf_multi = jnp.einsum(
        "bri,vbi->brv", leaf_basis, samples, preferred_element_type=jnp.float32
    ).astype(jnp.bfloat16)
    mid_multi = lift(transfer0, leaf_multi, rank_size, vector_count).astype(jnp.bfloat16)
    upper_multi = lift(transfer1, mid_multi, rank_size, vector_count).astype(jnp.bfloat16)
    leaf_flat = leaf_multi.reshape(leaf_boxes, block_width)
    mid_flat = mid_multi.reshape(mid_boxes, block_width)
    upper_flat = upper_multi.reshape(upper_boxes, block_width)
    leaf_requests, leaf_places = request_plan(lists0, leaf_boxes, leaf_room, own_index, devices)
    mid_requests, mid_places = request_plan(lists1, mid_boxes, mid_room, own_index, devices)
    upper_requests, upper_places = request_plan(lists2, upper_boxes, upper_room, own_index, devices)
    leaf_asked, mid_asked, upper_asked = (
        lax.all_to_all(leaf_requests, ("boxes", "grp"), split_axis=0, concat_axis=0, tiled=True),
        lax.all_to_all(mid_requests, ("boxes", "grp"), split_axis=0, concat_axis=0, tiled=True),
        lax.all_to_all(upper_requests, ("boxes", "grp"), split_axis=0, concat_axis=0, tiled=True),
    )
    leaf_send = serve(leaf_asked, leaf_flat)
    leaf_received = lax.all_to_all(
        leaf_send, ("boxes", "grp"), split_axis=0, concat_axis=0, tiled=True
    )
    leaf_local = far_field(
        extend(leaf_flat, leaf_received), leaf_places, kinds0, coupling[0], rank_size, vector_count
    )
    mid_send = serve(mid_asked, mid_flat)
    upper_send = serve(upper_asked, upper_flat)
    mid_received, upper_received = (
        lax.all_to_all(mid_send, ("boxes", "grp"), split_axis=0, concat_axis=0, tiled=True),
        lax.all_to_all(upper_send, ("boxes", "grp"), split_axis=0, concat_axis=0, tiled=True),
    )
    mid_table = extend(mid_flat, mid_received)
    upper_table = extend(upper_flat, upper_received)
    mid_local = far_field(mid_table, mid_places, kinds1, coupling[1], rank_size, vector_count)
    upper_local = far_field(upper_table, upper_places, kinds2, coupling[2], rank_size, vector_count)
    upper_matrices = transfer2.reshape(upper_boxes, rank_size, rank_size)
    kid_multi, kid_matrices = (
        lax.all_gather(upper_multi, "grp", axis=0, tiled=True),
        lax.all_gather(upper_matrices, "grp", axis=0, tiled=True),
    )
    coarse_multi = lift(kid_matrices, kid_multi, rank_size, vector_count).astype(jnp.bfloat16)
    coarse_whole = lax.all_gather(
        coarse_multi.reshape(-1, block_width), "boxes", axis=0, tiled=True
    )
    coarse_table, coarse_places = whole_table(coarse_whole, lists3)
    coarse_local = far_field(
        coarse_table, coarse_places, kinds3, coupling[3], rank_size, vector_count
    )
    coarse_field = coarse_local.astype(jnp.bfloat16)
    parent_index = (member * upper_boxes + jnp.arange(upper_boxes, dtype=jnp.int32)) // 8
    upper_parents = coarse_field[parent_index].reshape(upper_boxes, rank_size, vector_count)
    upper_field = lower(transfer2, upper_parents, upper_local, rank_size)
    mid_parents = jnp.repeat(upper_field.reshape(upper_boxes, rank_size, vector_count), 8, axis=0)
    mid_field = lower(transfer1, mid_parents, mid_local, rank_size)
    leaf_parents = jnp.repeat(mid_field.reshape(mid_boxes, rank_size, vector_count), 8, axis=0)
    leaf_field = lower(transfer0, leaf_parents, leaf_local, rank_size)
    potential = jnp.einsum(
        "bri,brv->vbi",
        leaf_basis,
        leaf_field.reshape(leaf_boxes, rank_size, vector_count),
        preferred_element_type=jnp.float32,
    )
    return potential.astype(jnp.bfloat16).reshape(vector_count, leaf_boxes * leaf_size)


def solution(mesh):
    in_specs = (
        P(None, ("boxes", "grp")),
        P(("boxes", "grp"), None, None),
        P(("boxes", "grp"), None),
        P(("boxes", "grp"), None),
        P(("boxes", "grp"), None),
        P(),
        P(("boxes", "grp"), None),
        P(("boxes", "grp"), None),
        P(("boxes", "grp"), None),
        P("boxes", None),
        P(("boxes", "grp"), None),
        P(("boxes", "grp"), None),
        P(("boxes", "grp"), None),
        P("boxes", None),
    )
    out_specs = P(None, ("boxes", "grp"))
    return jax.shard_map(
        on_device, mesh=mesh, in_specs=in_specs, out_specs=out_specs, check_vma=False
    )
```

profile of v0, /device:TPU:25, one launch (start us, length us, event | category | flops | bytes accessed | tf_op | source)
XLA Modules:
  0.0 1284.9 jit_solution(15853911163290044964)
XLA Ops:
  7.4 10.6 all-to-all-start.4
  18.9 14.6 %scatter_custom_fusion.2 = s32[2049]{0:T(1024)S(1)} fusion(s32[3024]{0:T(1024)S(1)} %bitcast.191, s32[3024]{0:T(1024)S(1)} %broadcast.381, s32[]{:T(128)} %copy.206), kind=kCustom, calls=%fused_computation.142 | custom fusion | bytes 8200 | tf_op jit(solution)/shard_map/scatter | solution.py:38
  42.4 112.2 %scatter_custom_fusion = s32[16385]{0:T(1024)S(1)} fusion(s32[24192]{0:T(1024)S(1)} %fusion.68, s32[24192]{0:T(1024)S(1)} %broadcast.380, s32[]{:T(128)} %copy.206), kind=kCustom, calls=%fused_computation.108 | custom fusion | bytes 65544 | tf_op jit(solution)/shard_map/scatter | solution.py:38
  160.5 8.4 scatter_custom_fusion.3
  170.2 60.4 %scatter_custom_fusion.1 = s32[4097]{0:T(1024)S(1)} fusion(s32[16384]{0:T(1024)S(1)} %compare_select_fusion.4, s32[16384]{0:T(1024)S(1)} %iota_bitcast_fusion, s32[]{:T(128)} %constant.125.clone.1), kind=kCustom, calls=%fused_computation.133 | custom fusion | bytes 16392 | tf_op jit(solution)/shard_map/scatter | solution.py:51
  231.3 9.8 all-to-all-start.2
  262.4 7.3 all-to-all-start.5
  288.1 30.4 %gather_fusion.4 = s32[3024]{0:T(1024)S(1)} fusion(s32[128,16]{0,1:T(8,128)S(1)} %get-tuple-element.166, s32[3024]{0:T(1024)S(1)} %reshape.540), kind=kCustom, calls=%fused_computation.4 | custom fusion | bytes 48384 | tf_op jit(solution)/shard_map/gather | solution.py:54
  319.4 18.2 %gather_fusion.2 = bf16[4096,1024]{1,0:T(8,128)(2,1)} fusion(bf16[128,1024]{1,0:T(8,128)(2,1)S(1)} %copy.116, s32[4096]{0:T(1024)S(1)} %broadcast_clamp_fusion), kind=kCustom, calls=%fused_computation.2 | custom fusion | bytes 16793600 | tf_op jit(solution)/shard_map/gather | solution.py:64
  346.1 10.2 all-to-all-start.1
  356.3 34.4 %fusion.95 = (bf16[1,316,4096]{2,0,1:T(2,128)(2,1)}, bf16[1,316,4096]{2,0,1:T(2,128)(2,1)}, bf16[1,316,4096]{2,0,1:T(2,128)(2,1)}, bf16[1,316,4096]{2,0,1:T(2,128)(2,1)}) fusion(bf16[4,316,4096]{2,0,1:T(4,128)(2,1)} %param.21), kind=kLoop, calls=%fused_computation.181 | loop fusion | bytes 20709376 | tf_op jit(solution)/shard_map/slice | solution.py:165
  390.7 11.2 copy.158
  406.9 11.2 copy.159
  418.2 26.6 %all_gather.9 = bf16[8,64,16]{1,2,0:T(8,128)(2,1)S(1)} all-gather(bf16[2,64,16]{1,2,0:T(8,128)(2,1)S(1)} %bitcast_reduce_fusion.1), channel_id=1, replica_groups=mesh['boxes'=32,'grp'=4] {'grp'}, dimensions={0}, use_global_device_ids=true | all-gather | bytes 20480 | tf_op jit(solution)/shard_map/all_gather | solution.py:156
  444.8 16.3 %all_gather.10 = bf16[8,64,64]{2,1,0:T(8,128)(2,1)S(1)} all-gather(bf16[2,64,64]{2,1,0:T(8,128)(2,1)S(1)} %reshape.500), channel_id=1, replica_groups=mesh['boxes'=32,'grp'=4] {'grp'}, dimensions={0}, use_global_device_ids=true | all-gather | bytes 81920 | tf_op jit(solution)/shard_map/all_gather | solution.py:157
  461.4 31.7 %all-gather = bf16[32,1,1024]{2,1,0:T(2,128)(2,1)S(1)} all-gather(bf16[1,1,1024]{2,1,0:T(2,128)(2,1)S(1)} %reshape.684), channel_id=1, replica_groups=mesh['boxes'=32,'grp'=4] {'boxes'}, dimensions={0}, use_global_device_ids=true | all-gather | bytes 67584 | tf_op jit(solution)/shard_map/all_gather | solution.py:160
  495.2 9.9 copy.160
  516.5 145.0 %gather_fusion.1 = s32[24192]{0:T(1024)S(1)} fusion(s32[128,128]{0,1:T(8,128)S(1)} %get-tuple-element.164, s32[24192]{0:T(1024)S(1)} %reshape.518), kind=kCustom, calls=%fused_computation.1 | custom fusion | bytes 387072 | tf_op jit(solution)/shard_map/gather | solution.py:54
  662.5 9.8 copy.157
  695.3 13.9 %gather_fusion.5 = bf16[3024,1024]{1,0:T(8,128)(2,1)} fusion(bf16[1041,1024]{1,0:T(8,128)(2,1)S(1)} %pad_maximum_fusion.1, s32[3072]{0:T(1024)S(1)} %pad_clamp_fusion.1), kind=kCustom, calls=%fused_computation.5 | custom fusion | bytes 12398400 | tf_op jit(solution)/shard_map/while/body/eval_jaxpr/gather | solution.py:16
  714.7 12.9 %fusion.12 = f32[16,316,1024]{1,2,0:T(8,128)} fusion(bf16[16,189,1024]{2,1,0:T(8,128)(2,1)} %reshape.547, s32[16,189]{1,0:T(8,128)S(1)} %copy-done.10), kind=kOutput, calls=%fused_computation.30 | convolution fusion | flops 1957991680 | bytes 26914624 | tf_op jit(solution)/shard_map/while/body/eval_jaxpr/bpk,bpc->bkc/dot_general | solution.py:18
  727.6 28.6 %fusion.26 = f32[16,16,64]{2,1,0:T(8,128)S(1)} fusion(f32[16,316,64,16]{1,3,2,0:T(8,128)} %bitcast.170, bf16[316,64,64]{0,2,1:T(8,128)(2,1)S(1)} %bitcast.174), kind=kOutput, calls=%fused_computation.49 | convolution fusion | flops 3976200192 | bytes 23363584 | tf_op jit(solution)/shard_map/while/body/eval_jaxpr/krs,bksv->brv/dot_general | solution.py:20
  757.0 7.3 pad_maximum_fusion
  764.3 514.6 %while.3 = (s32[]{:T(128)}, f32[8,16,64,16]{2,3,1,0:T(8,128)}, s32[8,16,189]{2,1,0:T(8,128)}, s32[8,16,189]{2,1,0:T(8,128)}, bf16[4225,1024]{1,0:T(8,128)(2,1)}, /*index=5*/f32[316,64,64]{0,1,2:T(8,128)}, s32[]{:T(128)}) while((s32[]{:T(128)}, f32[8,16,64,16]{2,3,1,0:T(8,128)}, s32[8,16,189]{2,1,0:T(8,128)}, ...), condition=%wide.region_4.5_spmd.clone, body=%wide.region_3.4_spmd.clone.sunk | while | flops 5934203904 | bytes 101145544 | solution.py:22
  765.4 20.4 %gather_fusion = bf16[3024,1024]{1,0:T(8,128)(2,1)} fusion(bf16[4225,1024]{1,0:T(8,128)(2,1)} %get-tuple-element.223, s32[3072]{0:T(1024)S(1)} %pad_clamp_fusion.6), kind=kCustom, calls=%fused_computation.clone.clone.1 | custom fusion | bytes 12398400 | tf_op jit(solution)/shard_map/while/body/eval_jaxpr/gather | solution.py:16
  792.1 13.1 %fusion.124 = f32[16,316,1024]{1,2,0:T(8,128)} fusion(bf16[16,189,1024]{2,1,0:T(8,128)(2,1)} %reshape.729, s32[16,189]{1,0:T(8,128)S(1)} %dynamic-slice_bitcast_fusion.2), kind=kOutput, calls=%fused_computation.20.clone.1 | convolution fusion | flops 1957991680 | bytes 26914624 | tf_op jit(solution)/shard_map/while/body/eval_jaxpr/bpk,bpc->bkc/dot_general | solution.py:18
  805.3 23.6 %fusion.125 = f32[8,16,64,16]{2,3,1,0:T(8,128)} fusion(f32[8,16,64,16]{2,3,1,0:T(8,128)} %get-tuple-element.213, s32[]{:T(128)} %get-tuple-element.212, f32[16,316,64,16]{1,3,2,0:T(8,128)} %bitcast.169, f32[316,64,64]{0,1,2:T(8,128)S(1)} %bitcast.172), kind=kOutput, calls=%fused_computation.23.clone.1 | convolution fusion | flops 3976200192 | bytes 30474752 | tf_op jit(solution)/shard_map/while/body/eval_jaxpr/krs,bksv->brv/dot_general | solution.py:20
  829.7 20.4 %gather_fusion = bf16[3024,1024]{1,0:T(8,128)(2,1)} fusion(bf16[4225,1024]{1,0:T(8,128)(2,1)} %get-tuple-element.223, s32[3072]{0:T(1024)S(1)} %pad_clamp_fusion.6), kind=kCustom, calls=%fused_computation.clone.clone.1 | custom fusion | bytes 12398400 | tf_op jit(solution)/shard_map/while/body/eval_jaxpr/gather | solution.py:16
  856.4 13.1 %fusion.124 = f32[16,316,1024]{1,2,0:T(8,128)} fusion(bf16[16,189,1024]{2,1,0:T(8,128)(2,1)} %reshape.729, s32[16,189]{1,0:T(8,128)S(1)} %dynamic-slice_bitcast_fusion.2), kind=kOutput, calls=%fused_computation.20.clone.1 | convolution fusion | flops 1957991680 | bytes 26914624 | tf_op jit(solution)/shard_map/while/body/eval_jaxpr/bpk,bpc->bkc/dot_general | solution.py:18
  869.6 23.6 %fusion.125 = f32[8,16,64,16]{2,3,1,0:T(8,128)} fusion(f32[8,16,64,16]{2,3,1,0:T(8,128)} %get-tuple-element.213, s32[]{:T(128)} %get-tuple-element.212, f32[16,316,64,16]{1,3,2,0:T(8,128)} %bitcast.169, f32[316,64,64]{0,1,2:T(8,128)S(1)} %bitcast.172), kind=kOutput, calls=%fused_computation.23.clone.1 | convolution fusion | flops 3976200192 | bytes 30474752 | tf_op jit(solution)/shard_map/while/body/eval_jaxpr/krs,bksv->brv/dot_general | solution.py:20
  894.0 20.4 %gather_fusion = bf16[3024,1024]{1,0:T(8,128)(2,1)} fusion(bf16[4225,1024]{1,0:T(8,128)(2,1)} %get-tuple-element.223, s32[3072]{0:T(1024)S(1)} %pad_clamp_fusion.6), kind=kCustom, calls=%fused_computation.clone.clone.1 | custom fusion | bytes 12398400 | tf_op jit(solution)/shard_map/while/body/eval_jaxpr/gather | solution.py:16
  920.7 13.1 %fusion.124 = f32[16,316,1024]{1,2,0:T(8,128)} fusion(bf16[16,189,1024]{2,1,0:T(8,128)(2,1)} %reshape.729, s32[16,189]{1,0:T(8,128)S(1)} %dynamic-slice_bitcast_fusion.2), kind=kOutput, calls=%fused_computation.20.clone.1 | convolution fusion | flops 1957991680 | bytes 26914624 | tf_op jit(solution)/shard_map/while/body/eval_jaxpr/bpk,bpc->bkc/dot_general | solution.py:18
  933.9 23.6 %fusion.125 = f32[8,16,64,16]{2,3,1,0:T(8,128)} fusion(f32[8,16,64,16]{2,3,1,0:T(8,128)} %get-tuple-element.213, s32[]{:T(128)} %get-tuple-element.212, f32[16,316,64,16]{1,3,2,0:T(8,128)} %bitcast.169, f32[316,64,64]{0,1,2:T(8,128)S(1)} %bitcast.172), kind=kOutput, calls=%fused_computation.23.clone.1 | convolution fusion | flops 3976200192 | bytes 30474752 | tf_op jit(solution)/shard_map/while/body/eval_jaxpr/krs,bksv->brv/dot_general | solution.py:20
  958.3 20.4 %gather_fusion = bf16[3024,1024]{1,0:T(8,128)(2,1)} fusion(bf16[4225,1024]{1,0:T(8,128)(2,1)} %get-tuple-element.223, s32[3072]{0:T(1024)S(1)} %pad_clamp_fusion.6), kind=kCustom, calls=%fused_computation.clone.clone.1 | custom fusion | bytes 12398400 | tf_op jit(solution)/shard_map/while/body/eval_jaxpr/gather | solution.py:16
  985.0 13.1 %fusion.124 = f32[16,316,1024]{1,2,0:T(8,128)} fusion(bf16[16,189,1024]{2,1,0:T(8,128)(2,1)} %reshape.729, s32[16,189]{1,0:T(8,128)S(1)} %dynamic-slice_bitcast_fusion.2), kind=kOutput, calls=%fused_computation.20.clone.1 | convolution fusion | flops 1957991680 | bytes 26914624 | tf_op jit(solution)/shard_map/while/body/eval_jaxpr/bpk,bpc->bkc/dot_general | solution.py:18
  998.2 23.6 %fusion.125 = f32[8,16,64,16]{2,3,1,0:T(8,128)} fusion(f32[8,16,64,16]{2,3,1,0:T(8,128)} %get-tuple-element.213, s32[]{:T(128)} %get-tuple-element.212, f32[16,316,64,16]{1,3,2,0:T(8,128)} %bitcast.169, f32[316,64,64]{0,1,2:T(8,128)S(1)} %bitcast.172), kind=kOutput, calls=%fused_computation.23.clone.1 | convolution fusion | flops 3976200192 | bytes 30474752 | tf_op jit(solution)/shard_map/while/body/eval_jaxpr/krs,bksv->brv/dot_general | solution.py:20
  1022.6 20.4 %gather_fusion = bf16[3024,1024]{1,0:T(8,128)(2,1)} fusion(bf16[4225,1024]{1,0:T(8,128)(2,1)} %get-tuple-element.223, s32[3072]{0:T(1024)S(1)} %pad_clamp_fusion.6), kind=kCustom, calls=%fused_computation.clone.clone.1 | custom fusion | bytes 12398400 | tf_op jit(solution)/shard_map/while/body/eval_jaxpr/gather | solution.py:16
  1049.3 13.1 %fusion.124 = f32[16,316,1024]{1,2,0:T(8,128)} fusion(bf16[16,189,1024]{2,1,0:T(8,128)(2,1)} %reshape.729, s32[16,189]{1,0:T(8,128)S(1)} %dynamic-slice_bitcast_fusion.2), kind=kOutput, calls=%fused_computation.20.clone.1 | convolution fusion | flops 1957991680 | bytes 26914624 | tf_op jit(solution)/shard_map/while/body/eval_jaxpr/bpk,bpc->bkc/dot_general | solution.py:18
  1062.5 23.6 %fusion.125 = f32[8,16,64,16]{2,3,1,0:T(8,128)} fusion(f32[8,16,64,16]{2,3,1,0:T(8,128)} %get-tuple-element.213, s32[]{:T(128)} %get-tuple-element.212, f32[16,316,64,16]{1,3,2,0:T(8,128)} %bitcast.169, f32[316,64,64]{0,1,2:T(8,128)S(1)} %bitcast.172), kind=kOutput, calls=%fused_computation.23.clone.1 | convolution fusion | flops 3976200192 | bytes 30474752 | tf_op jit(solution)/shard_map/while/body/eval_jaxpr/krs,bksv->brv/dot_general | solution.py:20
  1086.9 20.4 %gather_fusion = bf16[3024,1024]{1,0:T(8,128)(2,1)} fusion(bf16[4225,1024]{1,0:T(8,128)(2,1)} %get-tuple-element.223, s32[3072]{0:T(1024)S(1)} %pad_clamp_fusion.6), kind=kCustom, calls=%fused_computation.clone.clone.1 | custom fusion | bytes 12398400 | tf_op jit(solution)/shard_map/while/body/eval_jaxpr/gather | solution.py:16
  1113.6 13.1 %fusion.124 = f32[16,316,1024]{1,2,0:T(8,128)} fusion(bf16[16,189,1024]{2,1,0:T(8,128)(2,1)} %reshape.729, s32[16,189]{1,0:T(8,128)S(1)} %dynamic-slice_bitcast_fusion.2), kind=kOutput, calls=%fused_computation.20.clone.1 | convolution fusion | flops 1957991680 | bytes 26914624 | tf_op jit(solution)/shard_map/while/body/eval_jaxpr/bpk,bpc->bkc/dot_general | solution.py:18
  1126.7 23.6 %fusion.125 = f32[8,16,64,16]{2,3,1,0:T(8,128)} fusion(f32[8,16,64,16]{2,3,1,0:T(8,128)} %get-tuple-element.213, s32[]{:T(128)} %get-tuple-element.212, f32[16,316,64,16]{1,3,2,0:T(8,128)} %bitcast.169, f32[316,64,64]{0,1,2:T(8,128)S(1)} %bitcast.172), kind=kOutput, calls=%fused_computation.23.clone.1 | convolution fusion | flops 3976200192 | bytes 30474752 | tf_op jit(solution)/shard_map/while/body/eval_jaxpr/krs,bksv->brv/dot_general | solution.py:20
  1151.2 20.4 %gather_fusion = bf16[3024,1024]{1,0:T(8,128)(2,1)} fusion(bf16[4225,1024]{1,0:T(8,128)(2,1)} %get-tuple-element.223, s32[3072]{0:T(1024)S(1)} %pad_clamp_fusion.6), kind=kCustom, calls=%fused_computation.clone.clone.1 | custom fusion | bytes 12398400 | tf_op jit(solution)/shard_map/while/body/eval_jaxpr/gather | solution.py:16
  1177.9 13.1 %fusion.124 = f32[16,316,1024]{1,2,0:T(8,128)} fusion(bf16[16,189,1024]{2,1,0:T(8,128)(2,1)} %reshape.729, s32[16,189]{1,0:T(8,128)S(1)} %dynamic-slice_bitcast_fusion.2), kind=kOutput, calls=%fused_computation.20.clone.1 | convolution fusion | flops 1957991680 | bytes 26914624 | tf_op jit(solution)/shard_map/while/body/eval_jaxpr/bpk,bpc->bkc/dot_general | solution.py:18
  1191.0 23.6 %fusion.125 = f32[8,16,64,16]{2,3,1,0:T(8,128)} fusion(f32[8,16,64,16]{2,3,1,0:T(8,128)} %get-tuple-element.213, s32[]{:T(128)} %get-tuple-element.212, f32[16,316,64,16]{1,3,2,0:T(8,128)} %bitcast.169, f32[316,64,64]{0,1,2:T(8,128)S(1)} %bitcast.172), kind=kOutput, calls=%fused_computation.23.clone.1 | convolution fusion | flops 3976200192 | bytes 30474752 | tf_op jit(solution)/shard_map/while/body/eval_jaxpr/krs,bksv->brv/dot_general | solution.py:20
  1215.5 20.4 %gather_fusion = bf16[3024,1024]{1,0:T(8,128)(2,1)} fusion(bf16[4225,1024]{1,0:T(8,128)(2,1)} %get-tuple-element.223, s32[3072]{0:T(1024)S(1)} %pad_clamp_fusion.6), kind=kCustom, calls=%fused_computation.clone.clone.1 | custom fusion | bytes 12398400 | tf_op jit(solution)/shard_map/while/body/eval_jaxpr/gather | solution.py:16
  1242.2 13.1 %fusion.124 = f32[16,316,1024]{1,2,0:T(8,128)} fusion(bf16[16,189,1024]{2,1,0:T(8,128)(2,1)} %reshape.729, s32[16,189]{1,0:T(8,128)S(1)} %dynamic-slice_bitcast_fusion.2), kind=kOutput, calls=%fused_computation.20.clone.1 | convolution fusion | flops 1957991680 | bytes 26914624 | tf_op jit(solution)/shard_map/while/body/eval_jaxpr/bpk,bpc->bkc/dot_general | solution.py:18
  1255.3 23.6 %fusion.125 = f32[8,16,64,16]{2,3,1,0:T(8,128)} fusion(f32[8,16,64,16]{2,3,1,0:T(8,128)} %get-tuple-element.213, s32[]{:T(128)} %get-tuple-element.212, f32[16,316,64,16]{1,3,2,0:T(8,128)} %bitcast.169, f32[316,64,64]{0,1,2:T(8,128)S(1)} %bitcast.172), kind=kOutput, calls=%fused_computation.23.clone.1 | convolution fusion | flops 3976200192 | bytes 30474752 | tf_op jit(solution)/shard_map/while/body/eval_jaxpr/krs,bksv->brv/dot_general | solution.py:20
  (266 shorter events, 185.4 us)
Async XLA Ops:
  0.0 40.1 %copy-start.11 = (bf16[16,4096]{1,0:T(8,128)(2,1)S(1)}, bf16[16,4096]{1,0:T(8,128)(2,1)}, u32[]{:S(2)}) copy-start(bf16[16,4096]{1,0:T(8,128)(2,1)} %param.19) | copy-start | bytes 393220
  0.0 40.4 %copy-start.14 = (s32[128,189]{0,1:T(8,128)S(1)}, s32[128,189]{0,1:T(8,128)}, u32[]{:S(2)}) copy-start(s32[128,189]{0,1:T(8,128)} %param.22) | copy-start | bytes 290308
  7.4 223.9 %all-to-all-start.4 = ((s32[128,1,2]{2,1,0:T(1,128)}), s32[128,1,2]{2,1,0:T(1,128)S(1)}, u32[]{:S(2)}, u32[]{:S(2)}) async-start(s32[128,1,2]{2,1,0:T(1,128)} %bitcast.27), calls=%async_computation.4 | async-start | bytes 131072 | tf_op jit(solution)/shard_map/all_to_all | solution.py:135
  40.1 119.8 %copy-start = (bf16[128,64,64]{2,1,0:T(8,128)(2,1)}, bf16[128,64,64]{2,1,0:T(8,128)(2,1)S(1)}, u32[]{:S(2)}) copy-start(bf16[128,64,64]{2,1,0:T(8,128)(2,1)S(1)} %copy.120) | copy-start | bytes 3145732
  40.4 119.6 %copy-start.6 = (bf16[16,64,64]{2,1,0:T(8,128)(2,1)}, bf16[16,64,64]{2,1,0:T(8,128)(2,1)S(1)}, u32[]{:S(2)}) copy-start(bf16[16,64,64]{2,1,0:T(8,128)(2,1)S(1)} %reshape.493) | copy-start | bytes 393220
  40.5 119.5 %copy-start.8 = (s32[128,189]{1,0:T(8,128)}, s32[128,189]{1,0:T(8,128)S(1)}, u32[]{:S(2)}) copy-start(s32[128,189]{1,0:T(8,128)S(1)} %copy.101) | copy-start | bytes 290308
  231.3 17.2 %all-to-all-start.2 = ((s32[128,1,8]{2,1,0:T(1,128)}), s32[128,1,8]{2,1,0:T(1,128)S(1)}, u32[]{:S(2)}, u32[]{:S(2)}) async-start(s32[128,1,8]{2,1,0:T(1,128)} %bitcast.16), calls=%async_computation.2 | async-start | bytes 131072 | tf_op jit(solution)/shard_map/all_to_all | solution.py:134
  248.4 13.9 %all-to-all-start = ((s32[128,1,32]{2,1,0:T(1,128)}), s32[128,1,32]{2,1,0:T(1,128)S(1)}, u32[]{:S(2)}, u32[]{:S(2)}) async-start(s32[128,1,32]{2,1,0:T(1,128)} %bitcast.6), calls=%async_computation | async-start | bytes 131072 | tf_op jit(solution)/shard_map/all_to_all | solution.py:133
  262.4 18.6 %all-to-all-start.5 = ((bf16[128,2,1024]{2,1,0:T(2,128)(2,1)}), bf16[128,2,1024]{2,1,0:T(2,128)(2,1)}, u32[]{:S(2)}, u32[]{:S(2)}) async-start(bf16[128,2,1024]{2,1,0:T(2,128)(2,1)} %broadcast_select_fusion.1), calls=%async_computation.5 | async-start | bytes 1048576 | tf_op jit(solution)/shard_map/all_to_all | solution.py:148
  281.0 63.8 %all-to-all-start.3 = ((bf16[128,8,1024]{2,1,0:T(8,128)(2,1)}), bf16[128,8,1024]{2,1,0:T(8,128)(2,1)S(1)}, u32[]{:S(2)}, u32[]{:S(2)}) async-start(bf16[128,8,1024]{2,1,0:T(8,128)(2,1)} %bitcast_select_fusion), calls=%async_computation.3 | async-start | bytes 4194304 | tf_op jit(solution)/shard_map/all_to_all | solution.py:147
  288.1 30.6 %copy-start.15 = (s32[16,189]{1,0:T(8,128)S(1)}, s32[16,189]{1,0:T(8,128)}, u32[]{:S(2)}) copy-start(s32[16,189]{1,0:T(8,128)} %param.23) | copy-start | bytes 36292
  344.8 1.3 copy-start.4
  346.1 410.9 %all-to-all-start.1 = ((bf16[128,32,1024]{2,1,0:T(8,128)(2,1)}), bf16[128,32,1024]{2,1,0:T(8,128)(2,1)}, u32[]{:S(2)}, u32[]{:S(2)}) async-start(bf16[128,32,1024]{2,1,0:T(8,128)(2,1)} %broadcast_select_fusion), calls=%async_computation.1 | async-start | bytes 16777216 | tf_op jit(solution)/shard_map/all_to_all | solution.py:138
  390.7 15.5 %copy-start.16 = (s32[2,189]{1,0:T(2,128)S(1)}, s32[2,189]{1,0:T(2,128)}, u32[]{:S(2)}) copy-start(s32[2,189]{1,0:T(2,128)} %param.24) | copy-start | bytes 4540
  406.1 12.0 copy-start.17
  406.9 86.3 %copy-start.20 = (s32[1,189]{1,0:T(1,128)S(1)}, s32[1,189]{1,0:T(1,128)}, u32[]{:S(2)}) copy-start(s32[1,189]{1,0:T(1,128)} %param.25) | copy-start | bytes 2272
  672.2 6.2 copy-start.18
  672.2 6.2 copy-start.13
  681.6 5.4 copy-start.19
  684.7 4.4 copy-start.3
  687.1 7.8 copy-start.12
  687.1 8.0 copy-start.5
  709.2 5.5 copy-start.10
  714.7 12.9 %copy-start.2 = (bf16[1,316,4096]{1,2,0:T(8,128)(2,1)S(1)}, bf16[1,316,4096]{1,2,0:T(8,128)(2,1)}, u32[]{:S(2)}) copy-start(bf16[1,316,4096]{1,2,0:T(8,128)(2,1)} %copy.158) | copy-start | bytes 7766020
  727.6 28.6 %copy-start.7 = (bf16[16,64,64]{2,1,0:T(8,128)(2,1)S(1)}, bf16[16,64,64]{2,1,0:T(8,128)(2,1)}, u32[]{:S(2)}) copy-start(bf16[16,64,64]{2,1,0:T(8,128)(2,1)} %copy-done.6) | copy-start | bytes 393220
  764.3 514.6 %copy-start.9 = (bf16[16,64,16]{1,2,0:T(8,128)(2,1)S(1)}, bf16[16,64,16]{1,2,0:T(8,128)(2,1)}, u32[]{:S(2)}) copy-start(bf16[16,64,16]{1,2,0:T(8,128)(2,1)} %fusion.30) | copy-start | bytes 98308
  764.3 515.5 %copy-start.1 = (bf16[128,64,64]{2,1,0:T(8,128)(2,1)S(1)}, bf16[128,64,64]{2,1,0:T(8,128)(2,1)}, u32[]{:S(2)}) copy-start(bf16[128,64,64]{2,1,0:T(8,128)(2,1)} %copy-done) | copy-start | bytes 3145732
  791.3 14.0 %slice-start = ((s8[6291456]{0:T(1024)(128)(4,1)}), s8[4194304]{0:T(1024)(128)(4,1)S(1)}, s32[]{:S(2)}) async-start(s8[6291456]{0:T(1024)(128)(4,1)} %bitcast.171), calls=%async_computation.6 | async-start | bytes 8388608 | tf_op jit(solution)/shard_map/while
  792.1 13.1 %slice-start.1 = ((s8[6291456]{0:T(1024)(128)(4,1)}), s8[2097152]{0:T(1024)(128)(4,1)S(1)}, s32[]{:S(2)}) async-start(s8[6291456]{0:T(1024)(128)(4,1)} %bitcast.171), calls=%async_computation.7 | async-start | bytes 4194304 | tf_op jit(solution)/shard_map/while
  855.6 14.0 %slice-start = ((s8[6291456]{0:T(1024)(128)(4,1)}), s8[4194304]{0:T(1024)(128)(4,1)S(1)}, s32[]{:S(2)}) async-start(s8[6291456]{0:T(1024)(128)(4,1)} %bitcast.171), calls=%async_computation.6 | async-start | bytes 8388608 | tf_op jit(solution)/shard_map/while
  856.4 13.1 %slice-start.1 = ((s8[6291456]{0:T(1024)(128)(4,1)}), s8[2097152]{0:T(1024)(128)(4,1)S(1)}, s32[]{:S(2)}) async-start(s8[6291456]{0:T(1024)(128)(4,1)} %bitcast.171), calls=%async_computation.7 | async-start | bytes 4194304 | tf_op jit(solution)/shard_map/while
  919.8 14.0 %slice-start = ((s8[6291456]{0:T(1024)(128)(4,1)}), s8[4194304]{0:T(1024)(128)(4,1)S(1)}, s32[]{:S(2)}) async-start(s8[6291456]{0:T(1024)(128)(4,1)} %bitcast.171), calls=%async_computation.6 | async-start | bytes 8388608 | tf_op jit(solution)/shard_map/while
  920.7 13.1 %slice-start.1 = ((s8[6291456]{0:T(1024)(128)(4,1)}), s8[2097152]{0:T(1024)(128)(4,1)S(1)}, s32[]{:S(2)}) async-start(s8[6291456]{0:T(1024)(128)(4,1)} %bitcast.171), calls=%async_computation.7 | async-start | bytes 4194304 | tf_op jit(solution)/shard_map/while
  984.1 14.0 %slice-start = ((s8[6291456]{0:T(1024)(128)(4,1)}), s8[4194304]{0:T(1024)(128)(4,1)S(1)}, s32[]{:S(2)}) async-start(s8[6291456]{0:T(1024)(128)(4,1)} %bitcast.171), calls=%async_computation.6 | async-start | bytes 8388608 | tf_op jit(solution)/shard_map/while
  985.0 13.1 %slice-start.1 = ((s8[6291456]{0:T(1024)(128)(4,1)}), s8[2097152]{0:T(1024)(128)(4,1)S(1)}, s32[]{:S(2)}) async-start(s8[6291456]{0:T(1024)(128)(4,1)} %bitcast.171), calls=%async_computation.7 | async-start | bytes 4194304 | tf_op jit(solution)/shard_map/while
  1048.4 14.0 %slice-start = ((s8[6291456]{0:T(1024)(128)(4,1)}), s8[4194304]{0:T(1024)(128)(4,1)S(1)}, s32[]{:S(2)}) async-start(s8[6291456]{0:T(1024)(128)(4,1)} %bitcast.171), calls=%async_computation.6 | async-start | bytes 8388608 | tf_op jit(solution)/shard_map/while
  1049.3 13.1 %slice-start.1 = ((s8[6291456]{0:T(1024)(128)(4,1)}), s8[2097152]{0:T(1024)(128)(4,1)S(1)}, s32[]{:S(2)}) async-start(s8[6291456]{0:T(1024)(128)(4,1)} %bitcast.171), calls=%async_computation.7 | async-start | bytes 4194304 | tf_op jit(solution)/shard_map/while
  1112.7 14.0 %slice-start = ((s8[6291456]{0:T(1024)(128)(4,1)}), s8[4194304]{0:T(1024)(128)(4,1)S(1)}, s32[]{:S(2)}) async-start(s8[6291456]{0:T(1024)(128)(4,1)} %bitcast.171), calls=%async_computation.6 | async-start | bytes 8388608 | tf_op jit(solution)/shard_map/while
  1113.6 13.1 %slice-start.1 = ((s8[6291456]{0:T(1024)(128)(4,1)}), s8[2097152]{0:T(1024)(128)(4,1)S(1)}, s32[]{:S(2)}) async-start(s8[6291456]{0:T(1024)(128)(4,1)} %bitcast.171), calls=%async_computation.7 | async-start | bytes 4194304 | tf_op jit(solution)/shard_map/while
  1177.0 14.0 %slice-start = ((s8[6291456]{0:T(1024)(128)(4,1)}), s8[4194304]{0:T(1024)(128)(4,1)S(1)}, s32[]{:S(2)}) async-start(s8[6291456]{0:T(1024)(128)(4,1)} %bitcast.171), calls=%async_computation.6 | async-start | bytes 8388608 | tf_op jit(solution)/shard_map/while
  1177.9 13.1 %slice-start.1 = ((s8[6291456]{0:T(1024)(128)(4,1)}), s8[2097152]{0:T(1024)(128)(4,1)S(1)}, s32[]{:S(2)}) async-start(s8[6291456]{0:T(1024)(128)(4,1)} %bitcast.171), calls=%async_computation.7 | async-start | bytes 4194304 | tf_op jit(solution)/shard_map/while
  1241.3 14.0 %slice-start = ((s8[6291456]{0:T(1024)(128)(4,1)}), s8[4194304]{0:T(1024)(128)(4,1)S(1)}, s32[]{:S(2)}) async-start(s8[6291456]{0:T(1024)(128)(4,1)} %bitcast.171), calls=%async_computation.6 | async-start | bytes 8388608 | tf_op jit(solution)/shard_map/while
  1242.2 13.1 %slice-start.1 = ((s8[6291456]{0:T(1024)(128)(4,1)}), s8[2097152]{0:T(1024)(128)(4,1)S(1)}, s32[]{:S(2)}) async-start(s8[6291456]{0:T(1024)(128)(4,1)} %bitcast.171), calls=%async_computation.7 | async-start | bytes 4194304 | tf_op jit(solution)/shard_map/while
where the time goes:
time: 1300 us; the launch traced here: 1280 us
  local copies, waits for them, and re-layouts  750 us (58%)
  matrix products  362 us (28%)
  blocking collectives  74.6 us (6%)
  starting transfers between devices  50.8 us (4%)
  other arithmetic  30.1 us (2%)
  waiting for transfers between devices  16.6 us (1%)
    gather x21, local copies, waits for them, and re-layouts, one_block(): sources = extended[chosen]  232 us
    dot_general x11, matrix products, one_block(): jnp.einsum('krs,bksv->brv', couple_wide, grouped, precision=lax.Precision...  230 us
    gather x6, local copies, waits for them, and re-layouts, request_plan(): slot_index = slot_rank[owner_safe, within]  181 us
    scatter x3, local copies, waits for them, and re-layouts, request_plan(): needed = jnp.zeros((devices * box_count + 1,), jnp.int32).at[flat_index]....  130 us
    dot_general x11, matrix products, one_block(): jnp.einsum('bpk,bpc->bkc', selector, sources, preferred_element_type=jnp....  122 us
    scatter x3, local copies, waits for them, and re-layouts, request_plan(): requests = jnp.full((devices * capacity + 1,), -1, jnp.int32).at[target.r...  70.1 us
    unnamed x52, local copies, waits for them, and re-layouts  52.1 us
    slice x1, local copies, waits for them, and re-layouts, on_device(): coupling[3]  34.4 us
  transfers between devices with their start and end apart: 6, of which 3 were waited for; matrix products, arithmetic and copies ran while one was open for 47% of the time, Pallas kernels for 0%

commit v1 on v0

v1 whole, which is shorter than its diff:
```python
import functools

import jax
import jax.numpy as jnp
from jax import lax
from jax.experimental import pallas as pl
from jax.experimental.pallas import tpu as pltpu
from jax.sharding import PartitionSpec as P

BF = jnp.bfloat16
F32 = jnp.float32
I32 = jnp.int32
MESH = pl.DeviceIdType.MESH

DEV = 128
REACH = 13
SLOTS = 28
LEAFS = 128
ROOM = 32
SLOT_PAD = 192
TARGETS = 148
ZERO_ROW = SLOTS * LEAFS
MID_ROW = ZERO_ROW + 8
UPPER_ROW = MID_ROW + SLOTS * 16
COARSE_ROW = UPPER_ROW + SLOTS * 2
TABLE_ROWS = COARSE_ROW + 32
KIND_PAD = 320
VMEM = pl.BlockSpec(memory_space=pltpu.VMEM)
SMEM = pl.BlockSpec(memory_space=pltpu.SMEM)
NT = (((1,), (1,)), ((), ()))


def plan_kernel(l0, l1, l2, l3, k0, k1, k2, k3, rows_out, kinds_out, req_out):
    me = lax.axis_index("boxes") * 4 + lax.axis_index("grp")
    rows_out[...] = jnp.full(rows_out.shape, ZERO_ROW, I32)
    kinds_out[...] = jnp.zeros(kinds_out.shape, I32)
    start = 0
    for level, (lists, kinds, count, offset) in enumerate(
        ((l0, k0, 128, 0), (l1, k1, 16, MID_ROW), (l2, k2, 2, UPPER_ROW))
    ):
        ids = lists[...]
        whole = DEV * count
        rel = lax.rem(ids - (me - REACH) * count + whole, whole)
        far = (REACH + DEV // 2) * count
        rel = jnp.where(rel >= far, rel - far + (SLOTS - 1) * count, rel)
        rows_out[start : start + count, 0:189] = jnp.where(ids >= 0, rel + offset, ZERO_ROW)
        kinds_out[start : start + count, 0:189] = kinds[...] + level * KIND_PAD
        start += count
    ids = l3[...]
    rows_out[start : start + 1, 0:189] = jnp.where(ids >= 0, ids + COARSE_ROW, ZERO_ROW)
    kinds_out[start : start + 1, 0:189] = k3[...] + 3 * KIND_PAD

    sub_lo = lax.broadcasted_iota(I32, (LEAFS, SLOT_PAD), 0)
    sub_hi = lax.broadcasted_iota(I32, (32, SLOT_PAD), 0)

    def mark(t, seen):
        row = rows_out[pl.ds(t, 1), :]
        lo = jnp.where(sub_lo == (row & 127), 1.0, 0.0).astype(BF)
        hi = jnp.where(sub_hi == (row >> 7), 1.0, 0.0).astype(BF)
        return seen + lax.dot_general(hi, lo, NT, preferred_element_type=F32)

    seen = lax.fori_loop(0, LEAFS, mark, jnp.zeros((32, LEAFS), F32), unroll=4)
    needed = seen > 0.5
    lane = lax.broadcasted_iota(I32, (32, LEAFS), 1)
    upto = (
        lax.broadcasted_iota(I32, (LEAFS, LEAFS), 0) <= lax.broadcasted_iota(I32, (LEAFS, LEAFS), 1)
    )
    rank = jnp.dot(
        jnp.where(needed, 1.0, 0.0).astype(BF),
        jnp.where(upto, 1.0, 0.0).astype(BF),
        preferred_element_type=F32,
    )
    rank = jnp.where(needed, rank, 0.0)
    lane_f = lane.astype(F32)
    asked = jnp.zeros((32, LEAFS), F32)
    for q in range(ROOM):
        pick = jnp.sum(jnp.where(rank == q + 1.0, lane_f, 0.0), axis=1, keepdims=True)
        asked = jnp.where(lane == q, pick, asked)
    asked = asked.astype(I32)
    for h in range(SLOTS):
        req_out[h] = jnp.broadcast_to(asked[h : h + 1, :], (8, LEAFS))


def plan(lists, kinds):
    return pl.pallas_call(
        plan_kernel,
        out_shape=(
            jax.ShapeDtypeStruct((TARGETS, SLOT_PAD), I32),
            jax.ShapeDtypeStruct((TARGETS, SLOT_PAD), I32),
            jax.ShapeDtypeStruct((SLOTS, 8, 128), I32),
        ),
        in_specs=[VMEM] * 8,
        out_specs=[VMEM] * 3,
        compiler_params=pltpu.CompilerParams(vmem_limit_bytes=32 << 20),
        name="plan",
    )(*lists, *kinds)


def slot_of(i):
    return i + (i + 15) // 28


def offset_of(p):
    return p - REACH + (DEV // 2 - SLOTS + 1 + REACH) * (p // (SLOTS - 1))


def exchange_kernel(
    req, leaf, mu, part,
    leaf_out, mu_out, coarse_out,
    asked_v, asked_s, send, zbuf,
    req_ss, req_rs, loc_s, leaf_ss, leaf_rs, mu_ss, mu_rs, z_ss, z_rs, y_ss, y_rs, x_ss, x_rs,
):
    box = lax.axis_index("boxes")
    grp = lax.axis_index("grp")
    me = box * 4 + grp
    bx = box // 8
    by = box % 8

    def there(p):
        t = (me + offset_of(p) + DEV) % DEV
        return (t // 4, t % 4)

    def back(p):
        t = (me - offset_of(p) + DEV) % DEV
        return (t // 4, t % 4)

    def z_peer(i):
        return (box, (grp + i) % 4)

    def y_peer(i):
        return (bx * 8 + (by + i) % 8, grp)

    def x_peer(i):
        return (((bx + i) % 4) * 8 + by, grp)

    barrier = pltpu.get_barrier_semaphore()

    def greet(to, first, count):
        def one(i, c):
            pl.semaphore_signal(barrier, inc=1, device_id=to(i + first), device_id_type=MESH)
            return c

        lax.fori_loop(0, count, one, 0)

    greet(lambda i: there(slot_of(i)), 0, SLOTS - 1)
    greet(z_peer, 1, 3)
    greet(y_peer, 1, 7)
    greet(x_peer, 1, 3)
    pl.semaphore_wait(barrier, SLOTS - 1 + 13)

    def copy(src, dst, ss, rs, to):
        return pltpu.make_async_remote_copy(
            src_ref=src, dst_ref=dst, send_sem=ss, recv_sem=rs, device_id=to, device_id_type=MESH
        )

    def req_copy(p):
        return copy(req.at[p], asked_v.at[p], req_ss.at[p], req_rs.at[p], there(p))

    def leaf_copy(p):
        return copy(send.at[p], leaf_out.at[p], leaf_ss.at[p], leaf_rs.at[p], back(p))

    def mu_copy(p):
        return copy(mu, mu_out.at[p], mu_ss.at[p], mu_rs.at[p], back(p))

    def z_copy(i):
        return copy(part, zbuf.at[grp], z_ss.at[i], z_rs.at[i], z_peer(i))

    def y_copy(i):
        own = coarse_out.at[box]
        return copy(own, own, y_ss.at[i], y_rs.at[i], y_peer(i))

    def x_copy(i):
        own = coarse_out.at[pl.ds(bx * 8, 8)]
        return copy(own, own, x_ss.at[i], x_rs.at[i], x_peer(i))

    def each(count, first, act):
        def one(i, c):
            act(i + first)
            return c

        lax.fori_loop(0, count, one, 0)

    each(SLOTS - 1, 0, lambda i: req_copy(slot_of(i)).start())
    each(3, 1, lambda i: z_copy(i).start())
    each(SLOTS - 1, 0, lambda i: mu_copy(slot_of(i)).start())

    left = lax.broadcasted_iota(I32, (16, 128), 1) < 64

    def serve(i):
        p = slot_of(i)
        req_copy(p).wait_recv()
        local = pltpu.make_async_copy(asked_v.at[p], asked_s.at[p], loc_s.at[p])
        local.start()
        local.wait()
        for q in range(ROOM // 2):
            a = leaf[asked_s[p, 0, 2 * q]]
            b = leaf[asked_s[p, 0, 2 * q + 1]]
            send[p, q * 16 : (q + 1) * 16, :] = jnp.where(left, a, b)
        leaf_copy(p).start()

    each(SLOTS - 1, 0, serve)

    zbuf[grp] = part[...]
    each(3, 1, lambda i: z_copy(i).wait())
    coarse_out[box] = (zbuf[0] + zbuf[1] + zbuf[2] + zbuf[3]).astype(BF)
    each(7, 1, lambda i: y_copy(i).start())
    each(7, 1, lambda i: y_copy(i).wait())
    each(3, 1, lambda i: x_copy(i).start())
    each(3, 1, lambda i: x_copy(i).wait())

    each(SLOTS - 1, 0, lambda i: req_copy(slot_of(i)).wait_send())
    each(SLOTS - 1, 0, lambda i: mu_copy(slot_of(i)).wait())
    each(SLOTS - 1, 0, lambda i: leaf_copy(slot_of(i)).wait())


def exchange(req, leaf_twice, mu, part):
    sem = pltpu.SemaphoreType.DMA
    return pl.pallas_call(
        exchange_kernel,
        out_shape=(
            jax.ShapeDtypeStruct((SLOTS, 256, 128), BF),
            jax.ShapeDtypeStruct((SLOTS, 144, 128), BF),
            jax.ShapeDtypeStruct((32, 16, 128), BF),
        ),
        in_specs=[VMEM] * 4,
        out_specs=[VMEM] * 3,
        scratch_shapes=[
            pltpu.VMEM((SLOTS, 8, 128), I32),
            pltpu.SMEM((SLOTS, 8, 128), I32),
            pltpu.VMEM((SLOTS, 256, 128), BF),
            pltpu.VMEM((4, 16, 128), F32),
        ]
        + [sem((SLOTS,))] * 7
        + [sem((8,))] * 6,
        compiler_params=pltpu.CompilerParams(
            collective_id=0, has_side_effects=True, vmem_limit_bytes=32 << 20
        ),
        name="exchange",
    )(req, leaf_twice, mu, part)


def turn_kernel(coupling, out, rows):
    left = lax.broadcasted_iota(I32, (16, 128), 1) < 64
    for k in range(5):

        def spread(c, _, k=k):
            tile = coupling[0, k * 16 : (k + 1) * 16, pl.ds(pl.multiple_of(c * 128, 128), 128)]
            tile = tile.astype(F32)
            rows[pl.ds(k * 1024 + 2 * c, 16, stride=64), :] = jnp.where(left, tile, 0.0)
            rows[pl.ds(k * 1024 + 2 * c + 1, 16, stride=64), :] = jnp.where(left, 0.0, tile)
            return 0

        lax.fori_loop(0, 32, spread, 0, unroll=8)
    lane = lax.broadcasted_iota(I32, (32, 128), 1)
    low = jnp.where((lane & 31) == lax.broadcasted_iota(I32, (32, 128), 0), 1.0, 0.0).astype(BF)
    lower_half = (lax.broadcasted_iota(I32, (64, 128), 1) & 32) == 0

    def turn(i, _):
        parts = []
        for j in range(2):
            a = rows[pl.ds(pl.multiple_of((2 * i + j) * 64, 64), 64), :]
            parts += [jnp.where(lower_half, a, 0.0), jnp.where(lower_half, 0.0, a)]
        right = jnp.concatenate(parts, axis=0).astype(BF)
        w = lax.dot_general(low, right, NT, preferred_element_type=F32).astype(BF)
        out[2 * i] = w[:, :128]
        out[2 * i + 1] = w[:, 128:]
        return 0

    lax.fori_loop(0, 40, turn, 0, unroll=8)


def turn(coupling):
    return pl.pallas_call(
        turn_kernel,
        out_shape=jax.ShapeDtypeStruct((4 * KIND_PAD, 32, 128), BF),
        grid=(4, 4),
        in_specs=[pl.BlockSpec((1, 80, 4096), lambda i, j: (i, j, 0))],
        out_specs=pl.BlockSpec((80, 32, 128), lambda i, j: (i * 4 + j, 0, 0)),
        scratch_shapes=[pltpu.VMEM((80 * 64, 128), F32)],
        compiler_params=pltpu.CompilerParams(vmem_limit_bytes=32 << 20),
        name="turn",
    )(coupling)


def far_kernel(
    rows_idx, kinds_idx, req, own_leaf, own_mu, leaf_in, mu_in, coarse_in, weights, out, table
):
    l = lax.broadcasted_iota(I32, (128, 512), 0)
    n = lax.broadcasted_iota(I32, (128, 512), 1)
    spread = jnp.where(l == (n >> 7) * 32 + (n & 31), 1.0, 0.0).astype(BF)
    table[ZERO_ROW] = jnp.zeros((32, 128), BF)

    def fill(block, places):
        y = jnp.dot(block, spread, preferred_element_type=F32).astype(BF)
        for i, (a, b) in enumerate(places):
            s = slice(i * 16, (i + 1) * 16)
            table[a] = jnp.concatenate([y[s, 0:128], y[s, 128:256]], axis=0)
            if b is not None:
                table[b] = jnp.concatenate([y[s, 256:384], y[s, 384:512]], axis=0)

    def mu_places(p):
        mid = [(MID_ROW + p * 16 + 2 * i, MID_ROW + p * 16 + 2 * i + 1) for i in range(8)]
        return mid + [(UPPER_ROW + p * 2, UPPER_ROW + p * 2 + 1)]

    def peer(i, c):
        p = slot_of(i)
        fill(
            leaf_in[p],
            [(p * LEAFS + req[p, 0, 2 * q], p * LEAFS + req[p, 0, 2 * q + 1]) for q in range(16)],
        )
        fill(mu_in[p], mu_places(p))
        return c

    lax.fori_loop(0, SLOTS - 1, peer, 0)
    fill(own_mu[...], mu_places(REACH))

    def own(i, c):
        base = REACH * LEAFS + i * 32
        fill(
            own_leaf[pl.ds(pl.multiple_of(i * 256, 256), 256), :],
            [(base + 2 * q, base + 2 * q + 1) for q in range(16)],
        )
        return c

    lax.fori_loop(0, 4, own, 0)

    def coarse(i, c):
        fill(
            coarse_in[pl.ds(pl.multiple_of(i * 128, 128), 128), :],
            [(COARSE_ROW + i * 8 + q, None) for q in range(8)],
        )
        return c

    lax.fori_loop(0, 4, coarse, 0)

    lane = lax.broadcasted_iota(I32, (32, 128), 1)
    m1, m2, m3 = lane < 32, lane < 64, lane < 96
    left = lax.broadcasted_iota(I32, (16, 128), 1) < 64

    def merge(a, b, c, d):
        return jnp.where(m2, jnp.where(m1, a, b), jnp.where(m3, c, d))

    def one(t):
        acc = None
        for b in range(SLOT_PAD // 16):
            cols, quads = [], []
            for g in range(2):
                base = b * 16 + g * 8
                cols.append(
                    jnp.concatenate([weights[kinds_idx[t, base + j]] for j in range(8)], axis=0)
                )
                quads.append(
                    jnp.concatenate(
                        [
                            merge(*[table[rows_idx[t, base + q * 4 + i]] for i in range(4)])
                            for q in range(2)
                        ],
                        axis=1,
                    )
                )
            d = jnp.dot(
                jnp.concatenate(quads, axis=0),
                jnp.concatenate(cols, axis=1),
                preferred_element_type=F32,
            )
            acc = d if acc is None else acc + d
        u = jnp.where(
            left, acc[0:16, 0:128] + acc[32:48, 128:256], acc[16:32, 0:128] + acc[48:64, 128:256]
        )
        out[t] = (u + pltpu.roll(u, 64, 1))[:, :64]

    def four(i, c):
        for k in range(4):
            one(i * 4 + k)
        return c

    lax.fori_loop(0, TARGETS // 4, four, 0)


def far(rows_idx, kinds_idx, req, own_leaf, own_mu, leaf_in, mu_in, coarse_in, weights):
    return pl.pallas_call(
        far_kernel,
        out_shape=jax.ShapeDtypeStruct((TARGETS, 16, 64), F32),
        in_specs=[SMEM] * 3 + [VMEM] * 6,
        out_specs=VMEM,
        scratch_shapes=[pltpu.VMEM((TABLE_ROWS, 32, 128), BF)],
        compiler_params=pltpu.CompilerParams(vmem_limit_bytes=60 << 20),
        name="far",
    )(rows_idx, kinds_idx, req, own_leaf, own_mu, leaf_in, mu_in, coarse_in, weights)


def pairs(blocks):
    n = blocks.shape[0]
    return blocks.reshape(n // 2, 2, 16, 64).transpose(0, 2, 1, 3).reshape(n * 8, 128)


def lift(matrices, children):
    terms = jnp.einsum("bpc,bvc->bvp", matrices, children, preferred_element_type=F32)
    return terms


def lower(matrices, parents, local):
    terms = jnp.einsum("bpc,bvp->bvc", matrices, parents, preferred_element_type=F32)
    return (local + terms).astype(BF)


def on_device(
    charges, leaf_basis, transfer0, transfer1, transfer2, coupling,
    lists0, lists1, lists2, lists3, kinds0, kinds1, kinds2, kinds3,
):
    member = lax.axis_index("grp")
    samples = charges.reshape(16, 128, 256)
    e0 = transfer0.reshape(128, 64, 64)
    e1 = transfer1.reshape(16, 64, 64)
    e2 = transfer2.reshape(2, 64, 64)
    leaf = jnp.einsum("bri,vbi->bvr", leaf_basis, samples, preferred_element_type=F32).astype(BF)
    mid = lift(e0, leaf).reshape(16, 8, 16, 64).sum(axis=1).astype(BF)
    upper = lift(e1, mid).reshape(2, 8, 16, 64).sum(axis=1).astype(BF)
    part = lift(e2, upper).sum(axis=0)
    part = jnp.concatenate([part, jnp.zeros((16, 64), F32)], axis=1)
    leaf_twice = jnp.concatenate([leaf, leaf], axis=2)
    own_leaf = pairs(leaf)
    own_mu = jnp.concatenate([pairs(mid), pairs(upper)], axis=0)

    rows_idx, kinds_idx, req = plan(
        (lists0, lists1, lists2, lists3), (kinds0, kinds1, kinds2, kinds3)
    )
    leaf_in, mu_in, coarse_in = exchange(req, leaf_twice, own_mu, part)
    weights = turn(coupling)
    local = far(
        rows_idx, kinds_idx, req, own_leaf, own_mu, leaf_in, mu_in,
        coarse_in.reshape(512, 128), weights,
    )
    leaf_local = local[0:128]
    mid_local = local[128:144]
    upper_local = local[144:146]
    coarse_field = local[146:147].astype(BF)
    upper_field = lower(e2, jnp.repeat(coarse_field, 2, axis=0), upper_local)
    mid_field = lower(e1, jnp.repeat(upper_field, 8, axis=0), mid_local)
    leaf_field = lower(e0, jnp.repeat(mid_field, 8, axis=0), leaf_local)
    potential = jnp.einsum("bri,bvr->vbi", leaf_basis, leaf_field, preferred_element_type=F32)
    return potential.astype(BF).reshape(16, 128 * 256)


def solution(mesh):
    both = ("boxes", "grp")
    in_specs = (
        P(None, both),
        P(both, None, None),
        P(both, None),
        P(both, None),
        P(both, None),
        P(),
        P(both, None),
        P(both, None),
        P(both, None),
        P("boxes", None),
        P(both, None),
        P(both, None),
        P(both, None),
        P("boxes", None),
    )
    return jax.shard_map(
        on_device, mesh=mesh, in_specs=in_specs, out_specs=P(None, both), check_vma=False
    )
```

time: 1300 us -> 273 us (0.21)
  local copies, waits for them, and re-layouts: 750 us -> 44.3 us
  matrix products: 362 us -> 11 us
  Pallas kernels: 0 us -> 213 us
  blocking collectives: 74.6 us -> 0 us
  starting transfers between devices: 50.8 us -> 0 us
  other arithmetic: 30.1 us -> 0.29 us
  waiting for transfers between devices: 16.6 us -> 0 us
    gather x33 -> x0, local copies, waits for them, and re-layouts: 437 us -> none  [the longest x21 232 us: one_block(): sources = extended[chosen]]
    dot_general x29 -> x7, matrix products: 362 us -> 11 us  [the longest x1 3.87 us: on_device(): jnp.einsum('bri,bvr->vbi', leaf_basis, leaf_field, preferred_element_type...]
    pallas_call x0 -> x4, Pallas kernels: none -> 213 us  [the longest x1 99.6 us: far(): pl.pallas_call(far_kernel, out_shape=jax.ShapeDtypeStruct((TARGETS, 16, 6...]
    scatter x6 -> x0, local copies, waits for them, and re-layouts: 200 us -> none  [the longest x3 130 us: request_plan(): needed = jnp.zeros((devices * box_count + 1,), jnp.int32).at[flat_index]....]
    all_gather x3 -> x0, blocking collectives: 74.6 us -> none  [the longest x1 31.7 us: on_device(): lax.all_gather(coarse_multi.reshape(-1, block_width), 'boxes', axis=0, ti...]
    all_to_all x6 -> x0, starting transfers between devices: 50.8 us -> none  [the longest x1 10.6 us: on_device(): lax.all_to_all(upper_requests, ('boxes', 'grp'), split_axis=0, concat_axi...]
    slice x6 -> x0, local copies, waits for them, and re-layouts: 34.4 us -> none  [the longest x1 34.4 us: on_device(): coupling[3]]
    select_n x24 -> x0, other arithmetic: 20.8 us -> none  [the longest x3 10.1 us: serve(): return jnp.where((asked >= 0)[..., None], picked, jnp.zeros_like(picked))]
  transfers between devices with their start and end apart: 6 -> 0, of which waited for: 3 -> 0; matrix products, arithmetic and copies ran while one was open for 47% -> 0% of each run, Pallas kernels for 0% -> 0%
where the time goes in v1:
time: 273 us; the launch traced here: 268 us
  Pallas kernels  213 us (78%)
  local copies, waits for them, and re-layouts  44.3 us (16%)
  matrix products  11 us (4%)
    pallas_call x1, Pallas kernels, far(): pl.pallas_call(far_kernel, out_shape=jax.ShapeDtypeStruct((TARGETS, 16, 6...  99.6 us
    pallas_call x1, Pallas kernels, turn(): pl.pallas_call(turn_kernel, out_shape=jax.ShapeDtypeStruct((4 * KIND_PAD,...  57.9 us
    pallas_call x1, Pallas kernels, exchange(): pl.pallas_call(exchange_kernel, out_shape=(jax.ShapeDtypeStruct((SLOTS, 2...  48.1 us
    unnamed x39, local copies, waits for them, and re-layouts  33.1 us
    pallas_call x1, Pallas kernels, plan(): pl.pallas_call(plan_kernel, out_shape=(jax.ShapeDtypeStruct((TARGETS, SLO...  7.01 us

profile of v1, /device:TPU:25, one launch (start us, length us, event | category | flops | bytes accessed | tf_op | source)
XLA Modules:
  0.0 268.4 jit_solution(11985798188519600291)
XLA Ops:
  0.0 0.8 reshape.67
  0.8 1.0 copy.22.l0
  1.8 1.0 copy.23.k0
  2.8 0.0 copy-start.9
  2.8 0.7 copy-done.9
  3.5 0.7 copy-done.10
  4.2 0.7 copy-done.11
  4.9 0.7 copy-done.12
  5.6 0.7 copy-done.13
  6.3 0.7 copy-done.14
  7.0 7.0 %plan.1 = (s32[148,192]{1,0:T(8,128)S(1)}, s32[148,192]{1,0:T(8,128)S(1)}, s32[28,8,128]{2,1,0:T(8,128)S(1)}) custom-call(s32[128,189]{1,0:T(8,128)S(1)} %copy.22.l0, s32[16,189]{1,0:T(8,128)S(1)} %copy-done.9, s32[2,189]{1,0:T(2,128)S(1)} %copy-done.11, s32[1,189]{1,0:T(1,128)S(1)} %copy-done.13, s32[128,189]{1,0:T(8,128)S(1)} %copy.23.k0, ...), custom_call_target="tpu_custom_call" | custom-call | tf_op jit(solution)/shard_map/plan/pallas_call | solution.py:85
  14.0 0.0 copy-start.6
  14.0 0.6 copy-done.6
  14.6 1.3 reshape.64
  15.9 3.7 %convolution_convert_fusion.1 = bf16[128,16,64]{2,1,0:T(8,128)(2,1)S(1)} fusion(bf16[128,64,256]{2,1,0:T(8,128)(2,1)} %param.15, bf16[2,128,8,256]{3,2,1,0:T(8,128)(2,1)} %bitcast.51), kind=kOutput, calls=%fused_computation.3 | convolution fusion | flops 67239936 | bytes 5505024 | tf_op jit(solution)/shard_map/bri,vbi->bvr/dot_general | solution.py:416
  19.6 0.0 copy-done.7
  19.6 0.0 copy-start.15
  19.6 0.4 copy.40
  20.1 0.9 reshape.60.own_leaf
  21.0 0.3 pad_maximum_fusion.leaf
  21.3 0.0 copy-done.15
  21.3 1.3 copy.26
  22.6 3.9 %copy.27 = bf16[128,64,64]{2,1,0:T(8,128)(2,1)S(1)} copy(bf16[128,64,64]{0,2,1:T(8,128)(2,1)} %bitcast.48) | data formatting | bytes 2097152 | tf_op jit(solution)/shard_map/reshape | solution.py:413
  26.6 1.2 bitcast_reduce_fusion
  27.8 0.6 copy-done.16
  28.4 0.2 bitcast_reduce_fusion.1
  28.7 0.1 reshape.66
  28.8 0.1 convolution_bitcast_fusion
  28.9 0.9 copy.41
  29.8 0.1 reshape.63
  29.9 0.0 copy-done.4
  29.9 0.0 copy-start.5
  29.9 48.1 %exchange.1 = (bf16[28,256,128]{2,1,0:T(8,128)(2,1)S(1)}, bf16[28,144,128]{2,1,0:T(8,128)(2,1)S(1)}, bf16[32,16,128]{2,1,0:T(8,128)(2,1)S(1)}) custom-call(s32[28,8,128]{2,1,0:T(8,128)S(1)} %get-tuple-element.13.req, bf16[128,16,128]{2,1,0:T(8,128)(2,1)S(1)} %pad_maximum_fusion.leaf, bf16[144,128]{1,0:T(8,128)(2,1)S(1)} %constant_dynamic-update-slice_fusion.mu.own_mu, ...), custom_call_target="tpu_custom_call" | custom-call | tf_op jit(solution)/shard_map/exchange/pallas_call | solution.py:218
  78.0 1.2 copy-done.2
  79.2 1.0 copy-done.3
  80.2 0.7 copy-done.8
  80.9 13.6 %copy.30.coupling = bf16[4,316,4096]{2,1,0:T(8,128)(2,1)} copy(bf16[4,316,4096]{2,0,1:T(4,128)(2,1)} %param.19) | data formatting | bytes 20709376 | tf_op args[5]
  94.5 4.0 %copy-done.1 = bf16[4,316,4096]{2,1,0:T(8,128)(2,1)S(1)} copy-done((bf16[4,316,4096]{2,1,0:T(8,128)(2,1)S(1)}, bf16[4,316,4096]{2,1,0:T(8,128)(2,1)}, u32[]{:S(2)}) %copy-start.1) | copy-done | bytes 10354712
  98.4 57.9 %turn.1.weights = bf16[1280,32,128]{2,1,0:T(8,128)(2,1)S(1)} custom-call(bf16[4,316,4096]{2,1,0:T(8,128)(2,1)S(1)} %copy-done.1), custom_call_target="tpu_custom_call" | custom-call | tf_op jit(solution)/shard_map/turn/pallas_call | solution.py:273
  156.4 0.0 copy-start
  156.4 4.0 %copy-done = bf16[1280,32,128]{2,1,0:T(8,128)(2,1)} copy-done((bf16[1280,32,128]{2,1,0:T(8,128)(2,1)}, bf16[1280,32,128]{2,1,0:T(8,128)(2,1)S(1)}, u32[]{:S(2)}) %copy-start) | copy-done | bytes 10485784
  160.3 99.6 %far.1 = f32[148,16,64]{2,1,0:T(8,128)} custom-call(s32[148,192]{1,0:T(8,128)} %copy-done.6, s32[148,192]{1,0:T(8,128)} %copy-done.7, s32[28,8,128]{2,1,0:T(8,128)} %copy-done.4, bf16[1024,128]{1,0:T(8,128)(2,1)} %reshape.60.own_leaf, bf16[144,128]{1,0:T(8,128)(2,1)} %copy-done.5, bf16[28,256,128]{2,1,0:T(8,128)(2,1)} %copy-done.2, ...), custom_call_target="tpu_custom_call" | custom-call | tf_op jit(solution)/shard_map/far/pallas_call | solution.py:381
  259.9 0.7 fusion.7
  260.6 0.8 fusion.3
  261.5 1.1 fusion.2
  262.6 0.9 broadcast_in_dim.9
  263.5 3.9 %fusion = bf16[128,2,8,256]{3,2,1,0:T(8,128)(2,1)S(1)} fusion(bf16[128,64,256]{2,1,0:T(8,128)(2,1)} %param.15, bf16[128,16,64]{2,1,0:T(8,128)(2,1)} %bitcast.49, bf16[128,64,64]{2,1,0:T(8,128)(2,1)S(1)} %copy.27, f32[148,16,64]{2,1,0:T(8,128)} %far.1), kind=kOutput, calls=%fused_computation.1 | convolution fusion | flops 84672512 | bytes 7864320 | tf_op jit(solution)/shard_map/bri,bvr->vbi/dot_general | solution.py:441
  267.3 1.0 copy.33
  (18 shorter events, 0.1 us)
Async XLA Ops:
  2.8 0.7 copy-start.9
  3.5 0.7 copy-start.10
  4.2 0.7 copy-start.11
  4.9 0.7 copy-start.12
  5.6 0.7 copy-start.13
  6.3 0.7 copy-start.14
  14.0 0.6 copy-start.6
  14.6 5.0 %copy-start.7 = (s32[148,192]{1,0:T(8,128)}, s32[148,192]{1,0:T(8,128)S(1)}, u32[]{:S(2)}) copy-start(s32[148,192]{1,0:T(8,128)S(1)} %get-tuple-element.12.kinds_idx) | copy-start | bytes 340996
  14.6 15.3 %copy-start.4 = (s32[28,8,128]{2,1,0:T(8,128)}, s32[28,8,128]{2,1,0:T(8,128)S(1)}, u32[]{:S(2)}) copy-start(s32[28,8,128]{2,1,0:T(8,128)S(1)} %get-tuple-element.13.req) | copy-start | bytes 344068
  19.6 1.7 copy-start.15
  27.8 0.6 copy-start.16
  29.9 64.5 %copy-start.5 = (bf16[144,128]{1,0:T(8,128)(2,1)}, bf16[144,128]{1,0:T(8,128)(2,1)S(1)}, u32[]{:S(2)}) copy-start(bf16[144,128]{1,0:T(8,128)(2,1)S(1)} %constant_dynamic-update-slice_fusion.mu.own_mu) | copy-start | bytes 110596
  78.0 1.2 copy-start.2
  79.2 1.0 copy-start.3
  80.2 0.7 copy-start.8
  94.4 4.0 %copy-start.1 = (bf16[4,316,4096]{2,1,0:T(8,128)(2,1)S(1)}, bf16[4,316,4096]{2,1,0:T(8,128)(2,1)}, u32[]{:S(2)}) copy-start(bf16[4,316,4096]{2,1,0:T(8,128)(2,1)} %copy.30.coupling) | copy-start | bytes 31064068
  156.4 4.0 %copy-start = (bf16[1280,32,128]{2,1,0:T(8,128)(2,1)}, bf16[1280,32,128]{2,1,0:T(8,128)(2,1)S(1)}, u32[]{:S(2)}) copy-start(bf16[1280,32,128]{2,1,0:T(8,128)(2,1)S(1)} %turn.1.weights) | copy-start | bytes 31457284

commit v2 on v1

--- a/solution.py
+++ b/solution.py
@@ -24,13 +24,17 @@
 UPPER_ROW = MID_ROW + SLOTS * 16
 COARSE_ROW = UPPER_ROW + SLOTS * 2
 TABLE_ROWS = COARSE_ROW + 32
-KIND_PAD = 320
+KINDS = 316
 VMEM = pl.BlockSpec(memory_space=pltpu.VMEM)
 SMEM = pl.BlockSpec(memory_space=pltpu.SMEM)
 NT = (((1,), (1,)), ((), ()))
 
 
-def plan_kernel(l0, l1, l2, l3, k0, k1, k2, k3, rows_out, kinds_out, req_out):
+def iota(shape, dim):
+    return lax.broadcasted_iota(I32, shape, dim)
+
+
+def plan_kernel(l0, l1, l2, l3, k0, k1, k2, k3, rows_flat, kinds_flat, req_out, rows_out, kinds_out):
     me = lax.axis_index("boxes") * 4 + lax.axis_index("grp")
     rows_out[...] = jnp.full(rows_out.shape, ZERO_ROW, I32)
     kinds_out[...] = jnp.zeros(kinds_out.shape, I32)
@@ -44,14 +48,17 @@
         far = (REACH + DEV // 2) * count
         rel = jnp.where(rel >= far, rel - far + (SLOTS - 1) * count, rel)
         rows_out[start : start + count, 0:189] = jnp.where(ids >= 0, rel + offset, ZERO_ROW)
-        kinds_out[start : start + count, 0:189] = kinds[...] + level * KIND_PAD
+        kinds_out[start : start + count, 0:189] = kinds[...] * 4 + level
         start += count
     ids = l3[...]
     rows_out[start : start + 1, 0:189] = jnp.where(ids >= 0, ids + COARSE_ROW, ZERO_ROW)
-    kinds_out[start : start + 1, 0:189] = k3[...] + 3 * KIND_PAD
-
-    sub_lo = lax.broadcasted_iota(I32, (LEAFS, SLOT_PAD), 0)
-    sub_hi = lax.broadcasted_iota(I32, (32, SLOT_PAD), 0)
+    kinds_out[start : start + 1, 0:189] = k3[...] * 4 + 3
+    for flat, tiled in ((rows_flat, rows_out), (kinds_flat, kinds_out)):
+        flat[pl.ds(0, TARGETS, stride=2), :] = tiled[:, 0:128]
+        flat[pl.ds(1, TARGETS, stride=2), 0 : SLOT_PAD - 128] = tiled[:, 128:SLOT_PAD]
+
+    sub_lo = iota((LEAFS, SLOT_PAD), 0)
+    sub_hi = iota((32, SLOT_PAD), 0)
 
     def mark(t, seen):
         row = rows_out[pl.ds(t, 1), :]
@@ -61,9 +68,9 @@
 
     seen = lax.fori_loop(0, LEAFS, mark, jnp.zeros((32, LEAFS), F32), unroll=4)
     needed = seen > 0.5
-    lane = lax.broadcasted_iota(I32, (32, LEAFS), 1)
+    lane = iota((32, LEAFS), 1)
     upto = (
-        lax.broadcasted_iota(I32, (LEAFS, LEAFS), 0) <= lax.broadcasted_iota(I32, (LEAFS, LEAFS), 1)
+        iota((LEAFS, LEAFS), 0) <= iota((LEAFS, LEAFS), 1)
     )
     rank = jnp.dot(
         jnp.where(needed, 1.0, 0.0).astype(BF),
@@ -85,17 +92,53 @@
     return pl.pallas_call(
         plan_kernel,
         out_shape=(
-            jax.ShapeDtypeStruct((TARGETS, SLOT_PAD), I32),
-            jax.ShapeDtypeStruct((TARGETS, SLOT_PAD), I32),
+            jax.ShapeDtypeStruct((2 * TARGETS, 128), I32),
+            jax.ShapeDtypeStruct((2 * TARGETS, 128), I32),
             jax.ShapeDtypeStruct((SLOTS, 8, 128), I32),
         ),
         in_specs=[VMEM] * 8,
         out_specs=[VMEM] * 3,
+        scratch_shapes=[pltpu.VMEM((TARGETS, SLOT_PAD), I32)] * 2,
         compiler_params=pltpu.CompilerParams(vmem_limit_bytes=32 << 20),
         name="plan",
     )(*lists, *kinds)
 
 
+def turn(coupling, weights, first, last):
+    eye = jnp.where(iota((128, 128), 0) == iota((128, 128), 1), 1.0, 0.0).astype(BF)
+    row, col = iota((256, 256), 0), iota((256, 256), 1)
+    fits = (col & 63) == 2 * ((row & 127) >> 2) + (row >> 7)
+    pick = [
+        jnp.where(fits & (((col >> 6) ^ h) == (row & 3)), 1.0, 0.0).astype(BF) for h in range(2)
+    ]
+    left = iota((32, 128), 1) < 64
+
+    def step(i, _):
+        rows = [[], []]
+        for j in range(2):
+            pair = coupling[pl.ds(i * 4 + 2 * j, 2)].reshape(256, 128)
+            t = lax.dot_general(eye, pair, NT, preferred_element_type=F32).astype(BF)
+            for k in range(2):
+                y = t[:, k * 128 : (k + 1) * 128]
+                for h in range(2):
+                    a = y[h * 32 : h * 32 + 32]
+                    b = y[64 + h * 32 : 64 + h * 32 + 32]
+                    rows[h].append(jnp.concatenate([a, b], axis=1))
+        half = [
+            jnp.dot(jnp.concatenate(rows[h], axis=0), pick[h], preferred_element_type=F32).astype(BF)
+            for h in range(2)
+        ]
+        for k in range(4):
+            for p in range(2):
+                a = half[0][k * 32 : k * 32 + 32, p * 128 : (p + 1) * 128]
+                b = half[1][k * 32 : k * 32 + 32, p * 128 : (p + 1) * 128]
+                weights[i * 4 + k, 2 * p] = jnp.where(left, a, b)
+                weights[i * 4 + k, 2 * p + 1] = jnp.where(left, b, a)
+        return 0
+
+    lax.fori_loop(first, last, step, 0)
+
+
 def slot_of(i):
     return i + (i + 15) // 28
 
@@ -105,8 +148,8 @@
 
 
 def exchange_kernel(
-    req, leaf, mu, part,
-    leaf_out, mu_out, coarse_out,
+    req, leaf, mu, part, coupling,
+    leaf_out, mu_out, coarse_out, weights,
     asked_v, asked_s, send, zbuf,
     req_ss, req_rs, loc_s, leaf_ss, leaf_rs, mu_ss, mu_rs, z_ss, z_rs, y_ss, y_rs, x_ss, x_rs,
 ):
@@ -184,7 +227,7 @@
     each(3, 1, lambda i: z_copy(i).start())
     each(SLOTS - 1, 0, lambda i: mu_copy(slot_of(i)).start())
 
-    left = lax.broadcasted_iota(I32, (16, 128), 1) < 64
+    left = iota((16, 128), 1) < 64
 
     def serve(i):
         p = slot_of(i)
@@ -204,8 +247,10 @@
     each(3, 1, lambda i: z_copy(i).wait())
     coarse_out[box] = (zbuf[0] + zbuf[1] + zbuf[2] + zbuf[3]).astype(BF)
     each(7, 1, lambda i: y_copy(i).start())
+    turn(coupling, weights, 0, 39)
     each(7, 1, lambda i: y_copy(i).wait())
     each(3, 1, lambda i: x_copy(i).start())
+    turn(coupling, weights, 39, 79)
     each(3, 1, lambda i: x_copy(i).wait())
 
     each(SLOTS - 1, 0, lambda i: req_copy(slot_of(i)).wait_send())
@@ -213,7 +258,7 @@
     each(SLOTS - 1, 0, lambda i: leaf_copy(slot_of(i)).wait())
 
 
-def exchange(req, leaf_twice, mu, part):
+def exchange(req, leaf_twice, mu, part, coupling):
     sem = pltpu.SemaphoreType.DMA
     return pl.pallas_call(
         exchange_kernel,
@@ -221,9 +266,10 @@
             jax.ShapeDtypeStruct((SLOTS, 256, 128), BF),
             jax.ShapeDtypeStruct((SLOTS, 144, 128), BF),
             jax.ShapeDtypeStruct((32, 16, 128), BF),
+            jax.ShapeDtypeStruct((KINDS, 4, 32, 128), BF),
         ),
-        in_specs=[VMEM] * 4,
-        out_specs=[VMEM] * 3,
+        in_specs=[VMEM] * 5,
+        out_specs=[VMEM] * 4,
         scratch_shapes=[
             pltpu.VMEM((SLOTS, 8, 128), I32),
             pltpu.SMEM((SLOTS, 8, 128), I32),
@@ -233,80 +279,42 @@
         + [sem((SLOTS,))] * 7
         + [sem((8,))] * 6,
         compiler_params=pltpu.CompilerParams(
-            collective_id=0, has_side_effects=True, vmem_limit_bytes=32 << 20
+            collective_id=0, has_side_effects=True, vmem_limit_bytes=50 << 20
         ),
         name="exchange",
-    )(req, leaf_twice, mu, part)
-
-
-def turn_kernel(coupling, out, rows):
-    left = lax.broadcasted_iota(I32, (16, 128), 1) < 64
-    for k in range(5):
-
-        def spread(c, _, k=k):
-            tile = coupling[0, k * 16 : (k + 1) * 16, pl.ds(pl.multiple_of(c * 128, 128), 128)]
-            tile = tile.astype(F32)
-            rows[pl.ds(k * 1024 + 2 * c, 16, stride=64), :] = jnp.where(left, tile, 0.0)
-            rows[pl.ds(k * 1024 + 2 * c + 1, 16, stride=64), :] = jnp.where(left, 0.0, tile)
-            return 0
-
-        lax.fori_loop(0, 32, spread, 0, unroll=8)
-    lane = lax.broadcasted_iota(I32, (32, 128), 1)
-    low = jnp.where((lane & 31) == lax.broadcasted_iota(I32, (32, 128), 0), 1.0, 0.0).astype(BF)
-    lower_half = (lax.broadcasted_iota(I32, (64, 128), 1) & 32) == 0
-
-    def turn(i, _):
-        parts = []
-        for j in range(2):
-            a = rows[pl.ds(pl.multiple_of((2 * i + j) * 64, 64), 64), :]
-            parts += [jnp.where(lower_half, a, 0.0), jnp.where(lower_half, 0.0, a)]
-        right = jnp.concatenate(parts, axis=0).astype(BF)
-        w = lax.dot_general(low, right, NT, preferred_element_type=F32).astype(BF)
-        out[2 * i] = w[:, :128]
-        out[2 * i + 1] = w[:, 128:]
-        return 0
-
-    lax.fori_loop(0, 40, turn, 0, unroll=8)
-
-
-def turn(coupling):
-    return pl.pallas_call(
-        turn_kernel,
-        out_shape=jax.ShapeDtypeStruct((4 * KIND_PAD, 32, 128), BF),
-        grid=(4, 4),
-        in_specs=[pl.BlockSpec((1, 80, 4096), lambda i, j: (i, j, 0))],
-        out_specs=pl.BlockSpec((80, 32, 128), lambda i, j: (i * 4 + j, 0, 0)),
-        scratch_shapes=[pltpu.VMEM((80 * 64, 128), F32)],
-        compiler_params=pltpu.CompilerParams(vmem_limit_bytes=32 << 20),
-        name="turn",
-    )(coupling)
+    )(req, leaf_twice, mu, part, coupling)
 
 
 def far_kernel(
     rows_idx, kinds_idx, req, own_leaf, own_mu, leaf_in, mu_in, coarse_in, weights, out, table
 ):
-    l = lax.broadcasted_iota(I32, (128, 512), 0)
-    n = lax.broadcasted_iota(I32, (128, 512), 1)
+    l = iota((128, 512), 0)
+    n = iota((128, 512), 1)
     spread = jnp.where(l == (n >> 7) * 32 + (n & 31), 1.0, 0.0).astype(BF)
     table[ZERO_ROW] = jnp.zeros((32, 128), BF)
 
     def fill(block, places):
         y = jnp.dot(block, spread, preferred_element_type=F32).astype(BF)
-        for i, (a, b) in enumerate(places):
+        for i, (a, b, h) in enumerate(places):
             s = slice(i * 16, (i + 1) * 16)
-            table[a] = jnp.concatenate([y[s, 0:128], y[s, 128:256]], axis=0)
+            first = [y[s, 0:128], y[s, 128:256]]
+            table[a] = jnp.concatenate([first[h], first[1 - h]], axis=0)
             if b is not None:
-                table[b] = jnp.concatenate([y[s, 256:384], y[s, 384:512]], axis=0)
+                last = [y[s, 256:384], y[s, 384:512]]
+                table[b] = jnp.concatenate([last[h], last[1 - h]], axis=0)
 
     def mu_places(p):
-        mid = [(MID_ROW + p * 16 + 2 * i, MID_ROW + p * 16 + 2 * i + 1) for i in range(8)]
-        return mid + [(UPPER_ROW + p * 2, UPPER_ROW + p * 2 + 1)]
+        mid = [(MID_ROW + p * 16 + 2 * i, MID_ROW + p * 16 + 2 * i + 1, 1) for i in range(8)]
+        return mid + [(UPPER_ROW + p * 2, UPPER_ROW + p * 2 + 1, 0)]
 
     def peer(i, c):
         p = slot_of(i)
         fill(
             leaf_in[p],
-            [(p * LEAFS + req[p, 0, 2 * q], p * LEAFS + req[p, 0, 2 * q + 1]) for q in range(16)],
+            [
+                (p * LEAFS + req[p, 0, 2 * q], p * LEAFS + req[p, 0, 2 * q + 1], 0)
+                for q in range(16)
+            ],
         )
         fill(mu_in[p], mu_places(p))
         return c
@@ -318,7 +326,7 @@
         base = REACH * LEAFS + i * 32
         fill(
             own_leaf[pl.ds(pl.multiple_of(i * 256, 256), 256), :],
-            [(base + 2 * q, base + 2 * q + 1) for q in range(16)],
+            [(base + 2 * q, base + 2 * q + 1, 0) for q in range(16)],
         )
         return c
 
@@ -327,15 +335,15 @@
     def coarse(i, c):
         fill(
             coarse_in[pl.ds(pl.multiple_of(i * 128, 128), 128), :],
-            [(COARSE_ROW + i * 8 + q, None) for q in range(8)],
+            [(COARSE_ROW + i * 8 + q, None, 1) for q in range(8)],
         )
         return c
 
     lax.fori_loop(0, 4, coarse, 0)
 
-    lane = lax.broadcasted_iota(I32, (32, 128), 1)
+    lane = iota((32, 128), 1)
     m1, m2, m3 = lane < 32, lane < 64, lane < 96
-    left = lax.broadcasted_iota(I32, (16, 128), 1) < 64
+    left = iota((16, 128), 1) < 64
 
     def merge(a, b, c, d):
         return jnp.where(m2, jnp.where(m1, a, b), jnp.where(m3, c, d))
@@ -347,12 +355,12 @@
             for g in range(2):
                 base = b * 16 + g * 8
                 cols.append(
-                    jnp.concatenate([weights[kinds_idx[t, base + j]] for j in range(8)], axis=0)
+                    jnp.concatenate([weights[kinds_idx[t * 256 + base + j]] for j in range(8)], axis=0)
                 )
                 quads.append(
                     jnp.concatenate(
                         [
-                            merge(*[table[rows_idx[t, base + q * 4 + i]] for i in range(4)])
+                            merge(*[table[rows_idx[t * 256 + base + q * 4 + i]] for i in range(4)])
                             for q in range(2)
                         ],
                         axis=1,
@@ -425,11 +433,11 @@
     rows_idx, kinds_idx, req = plan(
         (lists0, lists1, lists2, lists3), (kinds0, kinds1, kinds2, kinds3)
     )
-    leaf_in, mu_in, coarse_in = exchange(req, leaf_twice, own_mu, part)
-    weights = turn(coupling)
+    by_kind = coupling.reshape(4, KINDS, 32, 128).transpose(1, 2, 0, 3).reshape(KINDS, 128, 128)
+    leaf_in, mu_in, coarse_in, weights = exchange(req, leaf_twice, own_mu, part, by_kind)
     local = far(
-        rows_idx, kinds_idx, req, own_leaf, own_mu, leaf_in, mu_in,
-        coarse_in.reshape(512, 128), weights,
+        rows_idx.reshape(-1), kinds_idx.reshape(-1), req, own_leaf, own_mu, leaf_in, mu_in,
+        coarse_in.reshape(512, 128), weights.reshape(4 * KINDS, 32, 128),
     )
     leaf_local = local[0:128]
     mid_local = local[128:144]

time: 273 us -> 199 us (0.73)
  Pallas kernels: 213 us -> 162 us
  local copies, waits for them, and re-layouts: 44.3 us -> 22.7 us
    pallas_call x2 -> x1, Pallas kernels: 64.9 us -> 7.02 us  [plan(): pl.pallas_call(plan_kernel, out_shape=(jax.ShapeDtypeStruct((2 * TARGETS,...]
    unnamed x39 -> x34, local copies, waits for them, and re-layouts: 33.1 us -> 11.6 us
    pallas_call x1, Pallas kernels: 48.1 us -> 67.2 us  [exchange(): pl.pallas_call(exchange_kernel, out_shape=(jax.ShapeDtypeStruct((SLOTS, 2...]
    pallas_call x1, Pallas kernels: 99.6 us -> 87.7 us  [far(): pl.pallas_call(far_kernel, out_shape=jax.ShapeDtypeStruct((TARGETS, 16, 6...]
where the time goes in v2:
time: 199 us; the launch traced here: 196 us
  Pallas kernels  162 us (81%)
  local copies, waits for them, and re-layouts  22.7 us (11%)
  matrix products  11 us (6%)
    pallas_call x1, Pallas kernels, far(): pl.pallas_call(far_kernel, out_shape=jax.ShapeDtypeStruct((TARGETS, 16, 6...  87.7 us
    pallas_call x1, Pallas kernels, exchange(): pl.pallas_call(exchange_kernel, out_shape=(jax.ShapeDtypeStruct((SLOTS, 2...  67.2 us
    unnamed x34, local copies, waits for them, and re-layouts  11.6 us
    pallas_call x1, Pallas kernels, plan(): pl.pallas_call(plan_kernel, out_shape=(jax.ShapeDtypeStruct((2 * TARGETS,...  7.02 us

profile of v2, /device:TPU:25, one launch (start us, length us, event | category | flops | bytes accessed | tf_op | source)
XLA Modules:
  0.0 196.2 jit_solution(4354089236139507579)
XLA Ops:
  0.0 0.8 reshape.84
  0.8 1.0 copy.22.l0
  1.8 1.0 copy.23.k0
  2.8 0.0 copy-start.7
  2.8 0.7 copy-done.7
  3.5 0.0 copy-start.8
  3.5 0.7 copy-done.8
  4.2 0.0 copy-start.9
  4.2 0.7 copy-done.9
  4.9 0.0 copy-start.10
  4.9 0.7 copy-done.10
  5.6 0.7 copy-done.11
  6.3 0.7 copy-done.12
  7.0 7.0 %plan.1 = (s32[296,128]{1,0:T(8,128)S(1)}, s32[296,128]{1,0:T(8,128)S(1)}, s32[28,8,128]{2,1,0:T(8,128)S(1)}) custom-call(s32[128,189]{1,0:T(8,128)S(1)} %copy.22.l0, s32[16,189]{1,0:T(8,128)S(1)} %copy-done.7, s32[2,189]{1,0:T(2,128)S(1)} %copy-done.9, s32[1,189]{1,0:T(1,128)S(1)} %copy-done.11, s32[128,189]{1,0:T(8,128)S(1)} %copy.23.k0, ...), custom_call_target="tpu_custom_call" | custom-call | tf_op jit(solution)/shard_map/plan/pallas_call | solution.py:92
  14.0 0.0 copy-start.4
  14.0 0.6 copy-done.4
  14.6 1.3 reshape.81
  15.9 3.7 %convolution_convert_fusion.1 = bf16[128,16,64]{2,1,0:T(8,128)(2,1)S(1)} fusion(bf16[128,64,256]{2,1,0:T(8,128)(2,1)} %param.15, bf16[2,128,8,256]{3,2,1,0:T(8,128)(2,1)} %bitcast.63), kind=kOutput, calls=%fused_computation.3 | convolution fusion | flops 67239936 | bytes 5505024 | tf_op jit(solution)/shard_map/bri,vbi->bvr/dot_general | solution.py:424
  19.6 0.0 copy-done.5
  19.6 0.0 copy-start.13
  19.7 0.4 copy.40
  20.1 1.0 reshape.77.own_leaf
  21.0 0.3 pad_maximum_fusion.leaf
  21.3 0.0 copy-done.13
  21.3 1.3 copy.26
  22.6 3.9 %copy.27 = bf16[128,64,64]{2,1,0:T(8,128)(2,1)S(1)} copy(bf16[128,64,64]{0,2,1:T(8,128)(2,1)} %bitcast.60) | data formatting | bytes 2097152 | tf_op jit(solution)/shard_map/reshape | solution.py:421
  26.6 1.2 bitcast_reduce_fusion
  27.8 0.6 copy-done.14
  28.4 0.2 bitcast_reduce_fusion.1
  28.7 0.1 reshape.83
  28.8 0.1 convolution_bitcast_fusion
  28.9 0.9 copy.41
  29.8 0.1 reshape.80
  29.9 0.0 copy-done.2
  30.0 0.0 copy-start.3
  30.0 67.2 %exchange.1 = (bf16[28,256,128]{2,1,0:T(8,128)(2,1)S(1)}, bf16[28,144,128]{2,1,0:T(8,128)(2,1)S(1)}, bf16[32,16,128]{2,1,0:T(8,128)(2,1)S(1)}, bf16[316,4,32,128]{3,2,1,0:T(8,128)(2,1)}) custom-call(s32[28,8,128]{2,1,0:T(8,128)S(1)} %get-tuple-element.14.req, bf16[128,16,128]{2,1,0:T(8,128)(2,1)S(1)} %pad_maximum_fusion.leaf, ...), custom_call_target="tpu_custom_call" | custom-call | tf_op jit(solution)/shard_map/exchange/pallas_call | solution.py:263
  97.2 0.0 copy-done.3
  97.2 0.0 copy-start
  97.2 1.2 copy-done
  98.4 1.0 copy-done.1
  99.4 0.7 copy-done.6
  100.1 87.7 %far.1 = f32[148,16,64]{2,1,0:T(8,128)} custom-call(s32[37888]{0:T(1024)} %bitcast.54, s32[37888]{0:T(1024)} %bitcast.55, s32[28,8,128]{2,1,0:T(8,128)} %copy-done.2, bf16[1024,128]{1,0:T(8,128)(2,1)} %reshape.77.own_leaf, bf16[144,128]{1,0:T(8,128)(2,1)} %copy-done.3, bf16[28,256,128]{2,1,0:T(8,128)(2,1)} %copy-done, bf16[28,144,128]{2,1,0:T(8,128)(2,1)} %copy-done.1, ...), custom_call_target="tpu_custom_call" | custom-call | tf_op jit(solution)/shard_map/far/pallas_call | solution.py:389
  187.8 0.7 fusion.7
  188.5 0.8 fusion.3
  189.4 1.1 fusion.2
  190.4 0.9 broadcast_in_dim.9
  191.3 3.9 %fusion = bf16[128,2,8,256]{3,2,1,0:T(8,128)(2,1)S(1)} fusion(bf16[128,64,256]{2,1,0:T(8,128)(2,1)} %param.15, bf16[128,16,64]{2,1,0:T(8,128)(2,1)} %bitcast.61, bf16[128,64,64]{2,1,0:T(8,128)(2,1)S(1)} %copy.27, f32[148,16,64]{2,1,0:T(8,128)} %far.1), kind=kOutput, calls=%fused_computation.1 | convolution fusion | flops 84672512 | bytes 7864320 | tf_op jit(solution)/shard_map/bri,bvr->vbi/dot_general | solution.py:449
  195.2 1.0 copy.33
  (12 shorter events, 0.1 us)
Async XLA Ops:
  2.8 0.7 copy-start.7
  3.5 0.7 copy-start.8
  4.2 0.7 copy-start.9
  4.9 0.7 copy-start.10
  5.6 0.7 copy-start.11
  6.3 0.7 copy-start.12
  14.0 0.6 copy-start.4
  14.6 5.0 %copy-start.5 = (s32[296,128]{1,0:T(8,128)}, s32[296,128]{1,0:T(8,128)S(1)}, u32[]{:S(2)}) copy-start(s32[296,128]{1,0:T(8,128)S(1)} %get-tuple-element.13) | copy-start | bytes 454660
  14.6 15.3 %copy-start.2 = (s32[28,8,128]{2,1,0:T(8,128)}, s32[28,8,128]{2,1,0:T(8,128)S(1)}, u32[]{:S(2)}) copy-start(s32[28,8,128]{2,1,0:T(8,128)S(1)} %get-tuple-element.14.req) | copy-start | bytes 344068
  19.6 1.7 copy-start.13
  27.8 0.6 copy-start.14
  30.0 67.3 %copy-start.3 = (bf16[144,128]{1,0:T(8,128)(2,1)}, bf16[144,128]{1,0:T(8,128)(2,1)S(1)}, u32[]{:S(2)}) copy-start(bf16[144,128]{1,0:T(8,128)(2,1)S(1)} %constant_dynamic-update-slice_fusion.mu.own_mu) | copy-start | bytes 110596
  97.2 1.2 copy-start
  98.4 1.0 copy-start.1
  99.4 0.7 copy-start.6

commit v3 on v2

--- a/solution.py
+++ b/solution.py
@@ -34,7 +34,7 @@
     return lax.broadcasted_iota(I32, shape, dim)
 
 
-def plan_kernel(l0, l1, l2, l3, k0, k1, k2, k3, rows_flat, kinds_flat, req_out, rows_out, kinds_out):
+def plan_kernel(l0, l1, l2, l3, k0, k1, k2, k3, rows_flat, kinds_flat, req_out, meta, rows_out, kinds_out):
     me = lax.axis_index("boxes") * 4 + lax.axis_index("grp")
     rows_out[...] = jnp.full(rows_out.shape, ZERO_ROW, I32)
     kinds_out[...] = jnp.zeros(kinds_out.shape, I32)
@@ -57,6 +57,23 @@
         flat[pl.ds(0, TARGETS, stride=2), :] = tiled[:, 0:128]
         flat[pl.ds(1, TARGETS, stride=2), 0 : SLOT_PAD - 128] = tiled[:, 128:SLOT_PAD]
 
+    live = jnp.where(rows_out[...] != ZERO_ROW, 1.0, 0.0).astype(BF)
+    down = jnp.dot(live, jnp.ones((SLOT_PAD, 256), BF), preferred_element_type=F32)[:, :TARGETS]
+    across = lax.dot_general(jnp.ones((8, SLOT_PAD), BF), live, NT, preferred_element_type=F32)
+    down = (down.astype(I32) + 15) >> 4
+    across = (across[0:1].astype(I32) + 15) >> 4
+    t_down, t_across = iota((TARGETS, TARGETS), 0), iota((TARGETS, TARGETS), 1)
+    before = (across > down) | ((across == down) & (t_across < t_down))
+    place = jnp.sum(jnp.where(before, 1.0, 0.0), axis=1, keepdims=True)
+    here = place == t_across.astype(F32)
+    order = jnp.sum(jnp.where(here, t_down.astype(F32), 0.0), axis=0, keepdims=True).astype(I32)
+    meta[...] = jnp.zeros(meta.shape, I32)
+    meta[0:1, 0:TARGETS] = order
+    sub = iota((16, TARGETS), 0)
+    over = jnp.sum(jnp.where(across > sub, 1.0, 0.0), axis=1, keepdims=True).astype(I32)
+    ends = jnp.where(iota((16, 256), 1) == iota((16, 256), 0), (over + 3) >> 2, 0)
+    meta[1:2, :] = jnp.sum(ends, axis=0, keepdims=True)
+
     sub_lo = iota((LEAFS, SLOT_PAD), 0)
     sub_hi = iota((32, SLOT_PAD), 0)
 
@@ -85,7 +102,7 @@
         asked = jnp.where(lane == q, pick, asked)
     asked = asked.astype(I32)
     for h in range(SLOTS):
-        req_out[h] = jnp.broadcast_to(asked[h : h + 1, :], (8, LEAFS))
+        req_out[h] = asked[h : h + 1, :]
 
 
 def plan(lists, kinds):
@@ -94,10 +111,11 @@
         out_shape=(
             jax.ShapeDtypeStruct((2 * TARGETS, 128), I32),
             jax.ShapeDtypeStruct((2 * TARGETS, 128), I32),
-            jax.ShapeDtypeStruct((SLOTS, 8, 128), I32),
+            jax.ShapeDtypeStruct((SLOTS, 1, 128), I32),
+            jax.ShapeDtypeStruct((8, 256), I32),
         ),
         in_specs=[VMEM] * 8,
-        out_specs=[VMEM] * 3,
+        out_specs=[VMEM] * 4,
         scratch_shapes=[pltpu.VMEM((TARGETS, SLOT_PAD), I32)] * 2,
         compiler_params=pltpu.CompilerParams(vmem_limit_bytes=32 << 20),
         name="plan",
@@ -229,12 +247,15 @@
 
     left = iota((16, 128), 1) < 64
 
+    turn(coupling, weights, 0, 6)
+    asked_v[REACH] = jnp.zeros((1, 128), I32)
+    each(SLOTS - 1, 0, lambda i: req_copy(slot_of(i)).wait_recv())
+    local = pltpu.make_async_copy(asked_v, asked_s, loc_s.at[0])
+    local.start()
+    local.wait()
+
     def serve(i):
         p = slot_of(i)
-        req_copy(p).wait_recv()
-        local = pltpu.make_async_copy(asked_v.at[p], asked_s.at[p], loc_s.at[p])
-        local.start()
-        local.wait()
         for q in range(ROOM // 2):
             a = leaf[asked_s[p, 0, 2 * q]]
             b = leaf[asked_s[p, 0, 2 * q + 1]]
@@ -247,10 +268,10 @@
     each(3, 1, lambda i: z_copy(i).wait())
     coarse_out[box] = (zbuf[0] + zbuf[1] + zbuf[2] + zbuf[3]).astype(BF)
     each(7, 1, lambda i: y_copy(i).start())
-    turn(coupling, weights, 0, 39)
+    turn(coupling, weights, 6, 36)
     each(7, 1, lambda i: y_copy(i).wait())
     each(3, 1, lambda i: x_copy(i).start())
-    turn(coupling, weights, 39, 79)
+    turn(coupling, weights, 36, 79)
     each(3, 1, lambda i: x_copy(i).wait())
 
     each(SLOTS - 1, 0, lambda i: req_copy(slot_of(i)).wait_send())
@@ -271,8 +292,8 @@
         in_specs=[VMEM] * 5,
         out_specs=[VMEM] * 4,
         scratch_shapes=[
-            pltpu.VMEM((SLOTS, 8, 128), I32),
-            pltpu.SMEM((SLOTS, 8, 128), I32),
+            pltpu.VMEM((SLOTS, 1, 128), I32),
+            pltpu.SMEM((SLOTS, 1, 128), I32),
             pltpu.VMEM((SLOTS, 256, 128), BF),
             pltpu.VMEM((4, 16, 128), F32),
         ]
@@ -286,7 +307,7 @@
 
 
 def far_kernel(
-    rows_idx, kinds_idx, req, own_leaf, own_mu, leaf_in, mu_in, coarse_in, weights, out, table
+    rows_idx, kinds_idx, req, meta, own_leaf, own_mu, leaf_in, mu_in, coarse_in, weights, out, table
 ):
     l = iota((128, 512), 0)
     n = iota((128, 512), 1)
@@ -348,9 +369,9 @@
     def merge(a, b, c, d):
         return jnp.where(m2, jnp.where(m1, a, b), jnp.where(m3, c, d))
 
-    def one(t):
+    def one(t, batches):
         acc = None
-        for b in range(SLOT_PAD // 16):
+        for b in range(batches):
             cols, quads = [], []
             for g in range(2):
                 base = b * 16 + g * 8
@@ -377,24 +398,28 @@
         )
         out[t] = (u + pltpu.roll(u, 64, 1))[:, :64]
 
-    def four(i, c):
+    def four(i, c, batches):
         for k in range(4):
-            one(i * 4 + k)
+            one(meta[0, i * 4 + k], batches)
         return c
 
-    lax.fori_loop(0, TARGETS // 4, four, 0)
-
-
-def far(rows_idx, kinds_idx, req, own_leaf, own_mu, leaf_in, mu_in, coarse_in, weights):
+    first = 0
+    for batches in range(SLOT_PAD // 16, 5, -1):
+        last = meta[1, batches - 1] if batches > 6 else TARGETS // 4
+        lax.fori_loop(first, last, functools.partial(four, batches=batches), 0)
+        first = last
+
+
+def far(rows_idx, kinds_idx, req, meta, own_leaf, own_mu, leaf_in, mu_in, coarse_in, weights):
     return pl.pallas_call(
         far_kernel,
         out_shape=jax.ShapeDtypeStruct((TARGETS, 16, 64), F32),
-        in_specs=[SMEM] * 3 + [VMEM] * 6,
+        in_specs=[SMEM] * 4 + [VMEM] * 6,
         out_specs=VMEM,
         scratch_shapes=[pltpu.VMEM((TABLE_ROWS, 32, 128), BF)],
         compiler_params=pltpu.CompilerParams(vmem_limit_bytes=60 << 20),
         name="far",
-    )(rows_idx, kinds_idx, req, own_leaf, own_mu, leaf_in, mu_in, coarse_in, weights)
+    )(rows_idx, kinds_idx, req, meta, own_leaf, own_mu, leaf_in, mu_in, coarse_in, weights)
 
 
 def pairs(blocks):
@@ -430,13 +455,13 @@
     own_leaf = pairs(leaf)
     own_mu = jnp.concatenate([pairs(mid), pairs(upper)], axis=0)
 
-    rows_idx, kinds_idx, req = plan(
+    rows_idx, kinds_idx, req, meta = plan(
         (lists0, lists1, lists2, lists3), (kinds0, kinds1, kinds2, kinds3)
     )
     by_kind = coupling.reshape(4, KINDS, 32, 128).transpose(1, 2, 0, 3).reshape(KINDS, 128, 128)
     leaf_in, mu_in, coarse_in, weights = exchange(req, leaf_twice, own_mu, part, by_kind)
     local = far(
-        rows_idx.reshape(-1), kinds_idx.reshape(-1), req, own_leaf, own_mu, leaf_in, mu_in,
+        rows_idx.reshape(-1), kinds_idx.reshape(-1), req, meta, own_leaf, own_mu, leaf_in, mu_in,
         coarse_in.reshape(512, 128), weights.reshape(4 * KINDS, 32, 128),
     )
     leaf_local = local[0:128]

time: 199 us -> 182 us (0.915)
  Pallas kernels: 162 us -> 145 us
    pallas_call x1, Pallas kernels: 87.7 us -> 72.1 us  [far(): pl.pallas_call(far_kernel, out_shape=jax.ShapeDtypeStruct((TARGETS, 16, 6...]
where the time goes in v3:
time: 182 us; the launch traced here: 179 us
  Pallas kernels  145 us (80%)
  local copies, waits for them, and re-layouts  22.4 us (12%)
  matrix products  11.1 us (6%)
    pallas_call x1, Pallas kernels, far(): pl.pallas_call(far_kernel, out_shape=jax.ShapeDtypeStruct((TARGETS, 16, 6...  72.1 us
    pallas_call x1, Pallas kernels, exchange(): pl.pallas_call(exchange_kernel, out_shape=(jax.ShapeDtypeStruct((SLOTS, 2...  65.5 us
    unnamed x34, local copies, waits for them, and re-layouts  12.2 us
    pallas_call x1, Pallas kernels, plan(): pl.pallas_call(plan_kernel, out_shape=(jax.ShapeDtypeStruct((2 * TARGETS,...  7.32 us
    reshape x1, local copies, waits for them, and re-layouts, on_device(): e0 = transfer0.reshape(128, 64, 64)  3.94 us
    dot_general x1, matrix products, on_device(): jnp.einsum('bri,bvr->vbi', leaf_basis, leaf_field, preferred_element_type...  3.87 us
    dot_general x1, matrix products, on_device(): jnp.einsum('bri,vbi->bvr', leaf_basis, samples, preferred_element_type=F32)  3.7 us

profile of v3, /device:TPU:25, one launch (start us, length us, event | category | flops | bytes accessed | tf_op | source)
XLA Modules:
  0.0 178.8 jit_solution(1804072789033050638)
XLA Ops:
  0.0 0.8 reshape.84
  0.8 1.0 copy.22.l0
  1.8 1.0 copy.23.k0
  2.8 0.0 copy-start.7
  2.8 0.7 copy-done.7
  3.5 0.0 copy-start.8
  3.5 0.7 copy-done.8
  4.2 0.0 copy-start.10
  4.2 0.7 copy-done.10
  4.9 0.0 copy-start.11
  4.9 0.7 copy-done.11
  5.6 0.7 copy-done.12
  6.3 0.7 copy-done.13
  7.0 7.3 %plan.1 = (s32[296,128]{1,0:T(8,128)S(1)}, s32[296,128]{1,0:T(8,128)S(1)}, s32[28,1,128]{2,1,0:T(1,128)S(1)}, s32[8,256]{1,0:T(8,128)S(1)}) custom-call(s32[128,189]{1,0:T(8,128)S(1)} %copy.22.l0, s32[16,189]{1,0:T(8,128)S(1)} %copy-done.7, s32[2,189]{1,0:T(2,128)S(1)} %copy-done.10, s32[1,189]{1,0:T(1,128)S(1)} %copy-done.12, s32[128,189]{1,0:T(8,128)S(1)} %copy.23.k0, ...), custom_call_target="tpu_custom_call" | custom-call | tf_op jit(solution)/shard_map/plan/pallas_call | solution.py:109
  14.3 0.0 copy-start.3
  14.3 0.6 copy-done.3
  14.9 0.6 copy-done.4
  15.6 0.6 copy-done.9
  16.2 1.2 reshape.81
  17.4 3.7 %convolution_convert_fusion.1 = bf16[128,16,64]{2,1,0:T(8,128)(2,1)S(1)} fusion(bf16[128,64,256]{2,1,0:T(8,128)(2,1)} %param.15, bf16[2,128,8,256]{3,2,1,0:T(8,128)(2,1)} %bitcast.63), kind=kOutput, calls=%fused_computation.3 | convolution fusion | flops 67239936 | bytes 5505024 | tf_op jit(solution)/shard_map/bri,vbi->bvr/dot_general | solution.py:449
  21.1 0.0 copy-start.14
  21.1 0.4 copy.40
  21.5 1.0 reshape.77.own_leaf
  22.5 0.3 pad_maximum_fusion.leaf
  22.8 0.0 copy-done.14
  22.8 1.3 copy.26
  24.1 3.9 %copy.27 = bf16[128,64,64]{2,1,0:T(8,128)(2,1)S(1)} copy(bf16[128,64,64]{0,2,1:T(8,128)(2,1)} %bitcast.60) | data formatting | bytes 2097152 | tf_op jit(solution)/shard_map/reshape | solution.py:446
  28.0 1.2 bitcast_reduce_fusion
  29.2 0.2 bitcast_reduce_fusion.1
  29.5 0.1 reshape.83
  29.6 0.1 convolution_bitcast_fusion
  29.7 0.1 copy.41
  29.8 0.1 reshape.80
  29.9 0.0 copy-done.6
  29.9 0.0 copy-start.2
  29.9 65.5 %exchange.1 = (bf16[28,256,128]{2,1,0:T(8,128)(2,1)S(1)}, bf16[28,144,128]{2,1,0:T(8,128)(2,1)S(1)}, bf16[32,16,128]{2,1,0:T(8,128)(2,1)S(1)}, bf16[316,4,32,128]{3,2,1,0:T(8,128)(2,1)}) custom-call(s32[28,1,128]{2,1,0:T(1,128)S(1)} %get-tuple-element.15.req, bf16[128,16,128]{2,1,0:T(8,128)(2,1)S(1)} %pad_maximum_fusion.leaf, ...), custom_call_target="tpu_custom_call" | custom-call | tf_op jit(solution)/shard_map/exchange/pallas_call | solution.py:284
  95.4 0.0 copy-done.2
  95.4 0.0 copy-start
  95.4 1.2 copy-done
  96.6 1.0 copy-done.1
  97.6 0.7 copy-done.5
  98.2 72.1 %far.1 = f32[148,16,64]{2,1,0:T(8,128)} custom-call(s32[37888]{0:T(1024)} %bitcast.54, s32[37888]{0:T(1024)} %bitcast.55, s32[28,1,128]{2,1,0:T(1,128)} %copy-done.6, s32[8,256]{1,0:T(8,128)} %copy-done.9, bf16[1024,128]{1,0:T(8,128)(2,1)} %reshape.77.own_leaf, bf16[144,128]{1,0:T(8,128)(2,1)} %copy-done.2, bf16[28,256,128]{2,1,0:T(8,128)(2,1)} %copy-done, ...), custom_call_target="tpu_custom_call" | custom-call | tf_op jit(solution)/shard_map/far/pallas_call | solution.py:414
  170.4 0.7 fusion.7
  171.1 0.8 fusion.3
  172.0 1.1 fusion.2
  173.0 0.9 broadcast_in_dim.9
  173.9 3.9 %fusion = bf16[128,2,8,256]{3,2,1,0:T(8,128)(2,1)S(1)} fusion(bf16[128,64,256]{2,1,0:T(8,128)(2,1)} %param.15, bf16[128,16,64]{2,1,0:T(8,128)(2,1)} %bitcast.61, bf16[128,64,64]{2,1,0:T(8,128)(2,1)S(1)} %copy.27, f32[148,16,64]{2,1,0:T(8,128)} %far.1), kind=kOutput, calls=%fused_computation.1 | convolution fusion | flops 84672512 | bytes 7864320 | tf_op jit(solution)/shard_map/bri,bvr->vbi/dot_general | solution.py:474
  177.8 1.0 copy.33
  (12 shorter events, 0.1 us)
Async XLA Ops:
  2.8 0.7 copy-start.7
  3.5 0.7 copy-start.8
  4.2 0.7 copy-start.10
  4.9 0.7 copy-start.11
  5.6 0.7 copy-start.12
  6.3 0.7 copy-start.13
  14.3 0.6 copy-start.3
  14.9 0.6 copy-start.4
  15.6 0.6 copy-start.9
  16.2 13.7 %copy-start.6 = (s32[28,1,128]{2,1,0:T(1,128)}, s32[28,1,128]{2,1,0:T(1,128)S(1)}, u32[]{:S(2)}) copy-start(s32[28,1,128]{2,1,0:T(1,128)S(1)} %get-tuple-element.15.req) | copy-start | bytes 43012
  21.1 1.7 copy-start.14
  29.9 65.5 %copy-start.2 = (bf16[144,128]{1,0:T(8,128)(2,1)}, bf16[144,128]{1,0:T(8,128)(2,1)S(1)}, u32[]{:S(2)}) copy-start(bf16[144,128]{1,0:T(8,128)(2,1)S(1)} %constant_dynamic-update-slice_fusion.mu.own_mu) | copy-start | bytes 110596
  95.4 1.2 copy-start
  96.6 1.0 copy-start.1
  97.6 0.7 copy-start.5

commit v4 on v3

--- a/solution.py
+++ b/solution.py
@@ -26,7 +26,9 @@
 TABLE_ROWS = COARSE_ROW + 32
 KINDS = 316
 VMEM = pl.BlockSpec(memory_space=pltpu.VMEM)
+ANY = pl.BlockSpec(memory_space=pl.ANY)
 SMEM = pl.BlockSpec(memory_space=pltpu.SMEM)
+TURN_PARTS = ((0, 10, 2), (10, 43, 3), (43, 79, 3))
 NT = (((1,), (1,)), ((), ()))
 
 
@@ -122,7 +124,51 @@
     )(*lists, *kinds)
 
 
-def turn(coupling, weights, first, last):
+def left_half():
+    return iota((16, 128), 1) < 64
+
+
+def lift(children, matrices):
+    left = left_half()
+    zero = jnp.zeros((16, 128), BF)
+    rows = [
+        jnp.concatenate([jnp.where(left, m, zero), jnp.where(left, zero, m)], axis=0)
+        for m in children
+    ]
+    return lax.dot_general(
+        jnp.concatenate(rows, axis=1),
+        jnp.concatenate(matrices, axis=1),
+        NT,
+        preferred_element_type=F32,
+    )
+
+
+def weave(split):
+    lane = iota((32, 128), 1) & 63
+    total = None
+    for h in range(2):
+        put = jnp.where(lane == 2 * iota((32, 128), 0) + h, 1.0, 0.0).astype(BF)
+        part = jnp.dot(split[h * 16 : (h + 1) * 16], put, preferred_element_type=F32)
+        total = part if total is None else total + part
+    return total.astype(BF)
+
+
+def unweave(block):
+    parts = []
+    for h in range(2):
+        row, lane = iota((128, 32), 0), iota((128, 32), 1)
+        put = jnp.where(row == 2 * lane + h, 1.0, 0.0).astype(BF)
+        parts.append(jnp.dot(block, put, preferred_element_type=F32))
+    return jnp.concatenate(parts, axis=0).astype(BF)
+
+
+def lowered(parent, matrix, local):
+    o = jnp.dot(parent, matrix, preferred_element_type=F32)
+    u = jnp.where(left_half(), o[0:16], o[16:32])
+    return (local + (u + pltpu.roll(u, 64, 1))).astype(BF)
+
+
+def turn(coupling, weights, first, last, per):
     eye = jnp.where(iota((128, 128), 0) == iota((128, 128), 1), 1.0, 0.0).astype(BF)
     row, col = iota((256, 256), 0), iota((256, 256), 1)
     fits = (col & 63) == 2 * ((row & 127) >> 2) + (row >> 7)
@@ -131,7 +177,7 @@
     ]
     left = iota((32, 128), 1) < 64
 
-    def step(i, _):
+    def group(i):
         rows = [[], []]
         for j in range(2):
             pair = coupling[pl.ds(i * 4 + 2 * j, 2)].reshape(256, 128)
@@ -152,9 +198,13 @@
                 b = half[1][k * 32 : k * 32 + 32, p * 128 : (p + 1) * 128]
                 weights[i * 4 + k, 2 * p] = jnp.where(left, a, b)
                 weights[i * 4 + k, 2 * p + 1] = jnp.where(left, b, a)
-        return 0
-
-    lax.fori_loop(first, last, step, 0)
+
+    def step(i, c):
+        for k in range(per):
+            group(first + i * per + k)
+        return c
+
+    lax.fori_loop(0, (last - first) // per, step, 0)
 
 
 def slot_of(i):
@@ -166,9 +216,10 @@
 
 
 def exchange_kernel(
-    req, leaf, mu, part, coupling,
-    leaf_out, mu_out, coarse_out, weights,
-    asked_v, asked_s, send, zbuf,
+    req, charges_any, basis_any, transfer, coupling_any,
+    leaf_out, mu_out, coarse_out, own_leaf, weights_any,
+    asked_v, asked_s, send, zbuf, coupling, weights, in_s, out_s,
+    charges, basis, leaf, mid, part,
     req_ss, req_rs, loc_s, leaf_ss, leaf_rs, mu_ss, mu_rs, z_ss, z_rs, y_ss, y_rs, x_ss, x_rs,
 ):
     box = lax.axis_index("boxes")
@@ -194,6 +245,13 @@
     def x_peer(i):
         return (((bx + i) % 4) * 8 + by, grp)
 
+    loads = [
+        pltpu.make_async_copy(charges_any, charges, in_s.at[0]),
+        pltpu.make_async_copy(basis_any, basis, in_s.at[1]),
+        pltpu.make_async_copy(coupling_any, coupling, in_s.at[2]),
+    ]
+    for load in loads:
+        load.start()
     barrier = pltpu.get_barrier_semaphore()
 
     def greet(to, first, count):
@@ -221,7 +279,7 @@
         return copy(send.at[p], leaf_out.at[p], leaf_ss.at[p], leaf_rs.at[p], back(p))
 
     def mu_copy(p):
-        return copy(mu, mu_out.at[p], mu_ss.at[p], mu_rs.at[p], back(p))
+        return copy(mu_out.at[REACH], mu_out.at[p], mu_ss.at[p], mu_rs.at[p], back(p))
 
     def z_copy(i):
         return copy(part, zbuf.at[grp], z_ss.at[i], z_rs.at[i], z_peer(i))
@@ -242,12 +300,38 @@
         lax.fori_loop(0, count, one, 0)
 
     each(SLOTS - 1, 0, lambda i: req_copy(slot_of(i)).start())
-    each(3, 1, lambda i: z_copy(i).start())
-    each(SLOTS - 1, 0, lambda i: mu_copy(slot_of(i)).start())
-
-    left = iota((16, 128), 1) < 64
-
-    turn(coupling, weights, 0, 6)
+    left = left_half()
+    loads[0].wait()
+    loads[1].wait()
+
+    def boxes(i, c):
+        blocks = []
+        for k in range(8):
+            b = i * 8 + k
+            w = basis[b]
+            points = charges[:, pl.ds(pl.multiple_of(b * 256, 256), 256)]
+            m = lax.dot_general(
+                points, jnp.concatenate([w, w], axis=0), NT, preferred_element_type=F32
+            ).astype(BF)
+            leaf[b] = m
+            blocks.append(m)
+        for k in range(4):
+            place = pl.ds(pl.multiple_of((i * 4 + k) * 16, 16), 16)
+            own_leaf[place, :] = jnp.where(left, blocks[2 * k], blocks[2 * k + 1])
+        return c
+
+    lax.fori_loop(0, LEAFS // 8, boxes, 0)
+
+
+    def turn_part(k):
+        first, last, per = TURN_PARTS[k]
+        turn(coupling, weights, first, last, per)
+        store_part(k).start()
+
+    def store_part(k):
+        span = pl.ds(TURN_PARTS[k][0] * 4, (TURN_PARTS[k][1] - TURN_PARTS[k][0]) * 4)
+        return pltpu.make_async_copy(weights.at[span], weights_any.at[span], out_s.at[k])
+
     asked_v[REACH] = jnp.zeros((1, 128), I32)
     each(SLOTS - 1, 0, lambda i: req_copy(slot_of(i)).wait_recv())
     local = pltpu.make_async_copy(asked_v, asked_s, loc_s.at[0])
@@ -264,22 +348,49 @@
 
     each(SLOTS - 1, 0, serve)
 
+    def mids(i, c):
+        for k in range(4):
+            t = i * 4 + k
+            mid[t] = weave(
+                lift([leaf[t * 8 + j] for j in range(8)], [transfer[t * 8 + j] for j in range(8)])
+                .astype(BF)
+            )
+        return c
+
+    lax.fori_loop(0, 4, mids, 0)
+    for q in range(8):
+        mu_out[REACH, q * 16 : (q + 1) * 16, :] = jnp.where(left, mid[2 * q], mid[2 * q + 1])
+    upper = []
+    for t in range(2):
+        children = range(t * 8, t * 8 + 8)
+        sums = lift([mid[j] for j in children], [transfer[128 + j] for j in children])
+        upper.append(weave(sums.astype(BF)))
+    mu_out[REACH, 128:144, :] = jnp.where(left, upper[0], upper[1])
+    part[...] = jnp.zeros(part.shape, F32)
+    part[:, 0:32] = lift(upper, [transfer[144], transfer[145]])
     zbuf[grp] = part[...]
+    each(3, 1, lambda i: z_copy(i).start())
+    each(SLOTS - 1, 0, lambda i: mu_copy(slot_of(i)).start())
+    loads[2].wait()
+    turn_part(0)
     each(3, 1, lambda i: z_copy(i).wait())
-    coarse_out[box] = (zbuf[0] + zbuf[1] + zbuf[2] + zbuf[3]).astype(BF)
+    whole = (zbuf[0] + zbuf[1] + zbuf[2] + zbuf[3]).astype(BF)
+    coarse_out[box] = weave(whole[:, 0:32])
     each(7, 1, lambda i: y_copy(i).start())
-    turn(coupling, weights, 6, 36)
+    turn_part(1)
     each(7, 1, lambda i: y_copy(i).wait())
     each(3, 1, lambda i: x_copy(i).start())
-    turn(coupling, weights, 36, 79)
+    turn_part(2)
     each(3, 1, lambda i: x_copy(i).wait())
 
     each(SLOTS - 1, 0, lambda i: req_copy(slot_of(i)).wait_send())
     each(SLOTS - 1, 0, lambda i: mu_copy(slot_of(i)).wait())
     each(SLOTS - 1, 0, lambda i: leaf_copy(slot_of(i)).wait())
-
-
-def exchange(req, leaf_twice, mu, part, coupling):
+    for k in range(len(TURN_PARTS)):
+        store_part(k).wait()
+
+
+def exchange(req, charges, basis, transfer, coupling):
     sem = pltpu.SemaphoreType.DMA
     return pl.pallas_call(
         exchange_kernel,
@@ -287,15 +398,25 @@
             jax.ShapeDtypeStruct((SLOTS, 256, 128), BF),
             jax.ShapeDtypeStruct((SLOTS, 144, 128), BF),
             jax.ShapeDtypeStruct((32, 16, 128), BF),
+            jax.ShapeDtypeStruct((1024, 128), BF),
             jax.ShapeDtypeStruct((KINDS, 4, 32, 128), BF),
         ),
-        in_specs=[VMEM] * 5,
-        out_specs=[VMEM] * 4,
+        in_specs=[VMEM, ANY, ANY, VMEM, ANY],
+        out_specs=[VMEM] * 4 + [ANY],
         scratch_shapes=[
             pltpu.VMEM((SLOTS, 1, 128), I32),
             pltpu.SMEM((SLOTS, 1, 128), I32),
             pltpu.VMEM((SLOTS, 256, 128), BF),
-            pltpu.VMEM((4, 16, 128), F32),
+            pltpu.VMEM((4, 32, 128), F32),
+            pltpu.VMEM((KINDS, 128, 128), BF),
+            pltpu.VMEM((KINDS, 4, 32, 128), BF),
+            sem((3,)),
+            sem((len(TURN_PARTS),)),
+            pltpu.VMEM((16, 32768), BF),
+            pltpu.VMEM((LEAFS, 64, 256), BF),
+            pltpu.VMEM((LEAFS, 16, 128), BF),
+            pltpu.VMEM((16, 16, 128), BF),
+            pltpu.VMEM((32, 128), F32),
         ]
         + [sem((SLOTS,))] * 7
         + [sem((8,))] * 6,
@@ -303,12 +424,18 @@
             collective_id=0, has_side_effects=True, vmem_limit_bytes=50 << 20
         ),
         name="exchange",
-    )(req, leaf_twice, mu, part, coupling)
+    )(req, charges, basis, transfer, coupling)
 
 
 def far_kernel(
-    rows_idx, kinds_idx, req, meta, own_leaf, own_mu, leaf_in, mu_in, coarse_in, weights, out, table
+    rows_idx, kinds_idx, req, meta, own_leaf, leaf_in, mu_in, coarse_in, transfer,
+    weights_any, basis_any, out,
+    table, weights, basis, local, parents, in_s,
 ):
+    load = pltpu.make_async_copy(weights_any, weights, in_s.at[0])
+    load_basis = pltpu.make_async_copy(basis_any, basis, in_s.at[1])
+    load.start()
+    load_basis.start()
     l = iota((128, 512), 0)
     n = iota((128, 512), 1)
     spread = jnp.where(l == (n >> 7) * 32 + (n & 31), 1.0, 0.0).astype(BF)
@@ -328,7 +455,12 @@
         mid = [(MID_ROW + p * 16 + 2 * i, MID_ROW + p * 16 + 2 * i + 1, 1) for i in range(8)]
         return mid + [(UPPER_ROW + p * 2, UPPER_ROW + p * 2 + 1, 0)]
 
-    def peer(i, c):
+    def peers(i, c):
+        for k in range(3):
+            peer(i * 3 + k)
+        return c
+
+    def peer(i):
         p = slot_of(i)
         fill(
             leaf_in[p],
@@ -338,10 +470,9 @@
             ],
         )
         fill(mu_in[p], mu_places(p))
-        return c
-
-    lax.fori_loop(0, SLOTS - 1, peer, 0)
-    fill(own_mu[...], mu_places(REACH))
+
+    lax.fori_loop(0, (SLOTS - 1) // 3, peers, 0)
+    fill(mu_in[REACH], mu_places(REACH))
 
     def own(i, c):
         base = REACH * LEAFS + i * 32
@@ -362,6 +493,7 @@
 
     lax.fori_loop(0, 4, coarse, 0)
 
+    load.wait()
     lane = iota((32, 128), 1)
     m1, m2, m3 = lane < 32, lane < 64, lane < 96
     left = iota((16, 128), 1) < 64
@@ -396,7 +528,7 @@
         u = jnp.where(
             left, acc[0:16, 0:128] + acc[32:48, 128:256], acc[16:32, 0:128] + acc[48:64, 128:256]
         )
-        out[t] = (u + pltpu.roll(u, 64, 1))[:, :64]
+        local[t] = u + pltpu.roll(u, 64, 1)
 
     def four(i, c, batches):
         for k in range(4):
@@ -409,70 +541,62 @@
         lax.fori_loop(first, last, functools.partial(four, batches=batches), 0)
         first = last
 
-
-def far(rows_idx, kinds_idx, req, meta, own_leaf, own_mu, leaf_in, mu_in, coarse_in, weights):
+    load_basis.wait()
+    coarse_field = unweave(local[146].astype(BF))
+    for u in range(2):
+        upper_field = unweave(lowered(coarse_field, transfer[144 + u], local[144 + u]))
+        for m in range(u * 8, u * 8 + 8):
+            parents[m] = unweave(lowered(upper_field, transfer[128 + m], local[128 + m]))
+
+    def boxes(m, c):
+        parent = parents[m]
+        for j in range(8):
+            b = m * 8 + j
+            field = lowered(parent, transfer[b], local[b])
+            points = jnp.dot(field[:, :64], basis[b], preferred_element_type=F32)
+            out[:, pl.ds(pl.multiple_of(b * 256, 256), 256)] = points.astype(BF)
+        return c
+
+    lax.fori_loop(0, 16, boxes, 0)
+
+
+def far(rows_idx, kinds_idx, req, meta, own_leaf, leaf_in, mu_in, coarse_in, transfer, weights, basis):
     return pl.pallas_call(
         far_kernel,
-        out_shape=jax.ShapeDtypeStruct((TARGETS, 16, 64), F32),
-        in_specs=[SMEM] * 4 + [VMEM] * 6,
+        out_shape=jax.ShapeDtypeStruct((16, LEAFS * 256), BF),
+        in_specs=[SMEM] * 4 + [VMEM] * 5 + [ANY] * 2,
         out_specs=VMEM,
-        scratch_shapes=[pltpu.VMEM((TABLE_ROWS, 32, 128), BF)],
+        scratch_shapes=[
+            pltpu.VMEM((TABLE_ROWS, 32, 128), BF),
+            pltpu.VMEM((4 * KINDS, 32, 128), BF),
+            pltpu.VMEM((LEAFS, 64, 256), BF),
+            pltpu.VMEM((TARGETS, 16, 128), F32),
+            pltpu.VMEM((16, 32, 32), BF),
+            pltpu.SemaphoreType.DMA((2,)),
+        ],
         compiler_params=pltpu.CompilerParams(vmem_limit_bytes=60 << 20),
         name="far",
-    )(rows_idx, kinds_idx, req, meta, own_leaf, own_mu, leaf_in, mu_in, coarse_in, weights)
-
-
-def pairs(blocks):
-    n = blocks.shape[0]
-    return blocks.reshape(n // 2, 2, 16, 64).transpose(0, 2, 1, 3).reshape(n * 8, 128)
-
-
-def lift(matrices, children):
-    terms = jnp.einsum("bpc,bvc->bvp", matrices, children, preferred_element_type=F32)
-    return terms
-
-
-def lower(matrices, parents, local):
-    terms = jnp.einsum("bpc,bvp->bvc", matrices, parents, preferred_element_type=F32)
-    return (local + terms).astype(BF)
+    )(
+        rows_idx, kinds_idx, req, meta, own_leaf, leaf_in, mu_in, coarse_in, transfer, weights, basis
+    )
 
 
 def on_device(
     charges, leaf_basis, transfer0, transfer1, transfer2, coupling,
     lists0, lists1, lists2, lists3, kinds0, kinds1, kinds2, kinds3,
 ):
-    member = lax.axis_index("grp")
-    samples = charges.reshape(16, 128, 256)
-    e0 = transfer0.reshape(128, 64, 64)
-    e1 = transfer1.reshape(16, 64, 64)
-    e2 = transfer2.reshape(2, 64, 64)
-    leaf = jnp.einsum("bri,vbi->bvr", leaf_basis, samples, preferred_element_type=F32).astype(BF)
-    mid = lift(e0, leaf).reshape(16, 8, 16, 64).sum(axis=1).astype(BF)
-    upper = lift(e1, mid).reshape(2, 8, 16, 64).sum(axis=1).astype(BF)
-    part = lift(e2, upper).sum(axis=0)
-    part = jnp.concatenate([part, jnp.zeros((16, 64), F32)], axis=1)
-    leaf_twice = jnp.concatenate([leaf, leaf], axis=2)
-    own_leaf = pairs(leaf)
-    own_mu = jnp.concatenate([pairs(mid), pairs(upper)], axis=0)
-
+    transfer = jnp.concatenate([transfer0, transfer1, transfer2], axis=0).reshape(146, 32, 128)
+    by_kind = coupling.reshape(4, KINDS, 32, 128).transpose(1, 2, 0, 3).reshape(KINDS, 128, 128)
     rows_idx, kinds_idx, req, meta = plan(
         (lists0, lists1, lists2, lists3), (kinds0, kinds1, kinds2, kinds3)
     )
-    by_kind = coupling.reshape(4, KINDS, 32, 128).transpose(1, 2, 0, 3).reshape(KINDS, 128, 128)
-    leaf_in, mu_in, coarse_in, weights = exchange(req, leaf_twice, own_mu, part, by_kind)
-    local = far(
-        rows_idx.reshape(-1), kinds_idx.reshape(-1), req, meta, own_leaf, own_mu, leaf_in, mu_in,
-        coarse_in.reshape(512, 128), weights.reshape(4 * KINDS, 32, 128),
-    )
-    leaf_local = local[0:128]
-    mid_local = local[128:144]
-    upper_local = local[144:146]
-    coarse_field = local[146:147].astype(BF)
-    upper_field = lower(e2, jnp.repeat(coarse_field, 2, axis=0), upper_local)
-    mid_field = lower(e1, jnp.repeat(upper_field, 8, axis=0), mid_local)
-    leaf_field = lower(e0, jnp.repeat(mid_field, 8, axis=0), leaf_local)
-    potential = jnp.einsum("bri,bvr->vbi", leaf_basis, leaf_field, preferred_element_type=F32)
-    return potential.astype(BF).reshape(16, 128 * 256)
+    leaf_in, mu_in, coarse_in, own_leaf, weights = exchange(
+        req, charges, leaf_basis, transfer, by_kind
+    )
+    return far(
+        rows_idx.reshape(-1), kinds_idx.reshape(-1), req, meta, own_leaf, leaf_in, mu_in,
+        coarse_in.reshape(512, 128), transfer, weights.reshape(4 * KINDS, 32, 128), leaf_basis,
+    )
 
 
 def solution(mesh):

time: 182 us -> 172 us (0.945); the launches traced: 179 us -> 172 us
  Pallas kernels: 145 us -> 161 us
  local copies, waits for them, and re-layouts: 22.4 us -> 9.61 us
  matrix products: 11.1 us -> 0 us
    pallas_call x1, Pallas kernels: 72.1 us -> 86.7 us  [far(): pl.pallas_call(far_kernel, out_shape=jax.ShapeDtypeStruct((16, LEAFS * 25...]
    dot_general x7 -> x0, matrix products: 11.1 us -> none  [the longest x1 3.87 us: on_device(): jnp.einsum('bri,bvr->vbi', leaf_basis, leaf_field, preferred_element_type...]
    reshape x8 -> x1, local copies, waits for them, and re-layouts: 8.54 us -> 0.21 us  [on_device(): jnp.concatenate([transfer0, transfer1, transfer2], axis=0)]
    unnamed x34 -> x33, local copies, waits for them, and re-layouts: 12.2 us -> 9.41 us
where the time goes in v4:
time: 172 us
  Pallas kernels  161 us (94%)
  local copies, waits for them, and re-layouts  9.61 us (6%)
    pallas_call x1, Pallas kernels, far(): pl.pallas_call(far_kernel, out_shape=jax.ShapeDtypeStruct((16, LEAFS * 25...  86.7 us
    pallas_call x1, Pallas kernels, exchange(): pl.pallas_call(exchange_kernel, out_shape=(jax.ShapeDtypeStruct((SLOTS, 2...  66.5 us
    unnamed x33, local copies, waits for them, and re-layouts  9.41 us
    pallas_call x1, Pallas kernels, plan(): pl.pallas_call(plan_kernel, out_shape=(jax.ShapeDtypeStruct((2 * TARGETS,...  7.32 us

profile of v4, /device:TPU:25, one launch (start us, length us, event | category | flops | bytes accessed | tf_op | source)
XLA Modules:
  0.0 172.0 jit_solution(15678678223394344776)
XLA Ops:
  0.0 1.0 copy.15.l0
  1.0 1.0 copy.16.k0
  2.0 0.0 copy-start.8
  2.0 0.7 copy-done.8
  2.7 0.0 copy-start.9
  2.7 0.7 copy-done.9
  3.4 0.0 copy-start.11
  3.4 0.7 copy-done.11
  4.1 0.0 copy-start.12
  4.1 0.7 copy-done.12
  4.8 0.0 copy-start.13
  4.8 0.7 copy-done.13
  5.5 0.0 copy-start.14
  5.5 0.7 copy-done.14
  6.2 7.3 %plan.1 = (s32[296,128]{1,0:T(8,128)S(1)}, s32[296,128]{1,0:T(8,128)S(1)}, s32[28,1,128]{2,1,0:T(1,128)S(1)}, s32[8,256]{1,0:T(8,128)S(1)}) custom-call(s32[128,189]{1,0:T(8,128)S(1)} %copy.15.l0, s32[16,189]{1,0:T(8,128)S(1)} %copy-done.8, s32[2,189]{1,0:T(2,128)S(1)} %copy-done.11, s32[1,189]{1,0:T(1,128)S(1)} %copy-done.13, s32[128,189]{1,0:T(8,128)S(1)} %copy.16.k0, ...), custom_call_target="tpu_custom_call" | custom-call | tf_op jit(solution)/shard_map/plan/pallas_call | solution.py:111
  13.5 0.0 copy-start.4
  13.5 0.0 copy-start.5
  13.5 0.0 copy-start.10
  13.5 0.0 copy-start.7
  13.5 1.5 pad_maximum_fusion
  15.0 0.0 copy-start.1
  15.1 0.2 copy.18
  15.3 0.0 copy-done.4
  15.3 0.0 copy-done.5
  15.3 0.0 copy-done.10
  15.3 0.2 slice.transfer
  15.6 0.0 copy-done.7
  15.6 0.7 copy-done.1
  16.3 0.0 copy-start
  16.3 66.5 %exchange.1 = (bf16[28,256,128]{2,1,0:T(8,128)(2,1)}, bf16[28,144,128]{2,1,0:T(8,128)(2,1)S(1)}, bf16[32,16,128]{2,1,0:T(8,128)(2,1)S(1)}, bf16[1024,128]{1,0:T(8,128)(2,1)S(1)}, bf16[316,4,32,128]{3,2,1,0:T(8,128)(2,1)}) custom-call(s32[28,1,128]{2,1,0:T(1,128)S(1)} %get-tuple-element.16.req, bf16[16,32768]{1,0:T(8,128)(2,1)S(1)} %copy-done.1, ...), custom_call_target="tpu_custom_call" | custom-call | tf_op jit(solution)/shard_map/exchange/pallas_call | solution.py:395
  82.8 0.0 copy-done
  82.8 0.0 copy-start.2
  82.8 1.0 copy-done.2
  83.8 0.0 copy-start.3
  83.8 0.7 copy-done.3
  84.5 0.0 copy-start.6
  84.5 0.6 copy-done.6
  85.1 86.7 %far.1 = bf16[16,32768]{1,0:T(8,128)(2,1)} custom-call(s32[37888]{0:T(1024)} %bitcast.12, s32[37888]{0:T(1024)} %bitcast.13, s32[28,1,128]{2,1,0:T(1,128)} %copy-done.7, s32[8,256]{1,0:T(8,128)} %copy-done.10, bf16[1024,128]{1,0:T(8,128)(2,1)} %copy-done.3, bf16[28,256,128]{2,1,0:T(8,128)(2,1)} %get-tuple-element.19.leaf_in, ...), custom_call_target="tpu_custom_call" | custom-call | tf_op jit(solution)/shard_map/far/pallas_call | solution.py:564
Async XLA Ops:
  2.0 0.7 copy-start.8
  2.7 0.7 copy-start.9
  3.4 0.7 copy-start.11
  4.1 0.7 copy-start.12
  4.8 0.7 copy-start.13
  5.5 0.7 copy-start.14
  13.5 1.8 %copy-start.4 = (s32[296,128]{1,0:T(8,128)}, s32[296,128]{1,0:T(8,128)S(1)}, u32[]{:S(2)}) copy-start(s32[296,128]{1,0:T(8,128)S(1)} %get-tuple-element.14) | copy-start | bytes 454660
  13.5 1.8 %copy-start.5 = (s32[296,128]{1,0:T(8,128)}, s32[296,128]{1,0:T(8,128)S(1)}, u32[]{:S(2)}) copy-start(s32[296,128]{1,0:T(8,128)S(1)} %get-tuple-element.15) | copy-start | bytes 454660
  13.5 1.8 %copy-start.10 = (s32[8,256]{1,0:T(8,128)}, s32[8,256]{1,0:T(8,128)S(1)}, u32[]{:S(2)}) copy-start(s32[8,256]{1,0:T(8,128)S(1)} %get-tuple-element.17.meta) | copy-start | bytes 24580
  13.5 2.0 %copy-start.7 = (s32[28,1,128]{2,1,0:T(1,128)}, s32[28,1,128]{2,1,0:T(1,128)S(1)}, u32[]{:S(2)}) copy-start(s32[28,1,128]{2,1,0:T(1,128)S(1)} %get-tuple-element.16.req) | copy-start | bytes 43012
  15.0 1.2 copy-start.1
  16.3 66.5 %copy-start = (bf16[146,32,128]{2,1,0:T(8,128)(2,1)}, bf16[146,32,128]{2,1,0:T(8,128)(2,1)S(1)}, u32[]{:S(2)}) copy-start(bf16[146,32,128]{2,1,0:T(8,128)(2,1)S(1)} %slice.transfer) | copy-start | bytes 3588100
  82.8 1.0 copy-start.2
  83.8 0.7 copy-start.3
  84.5 0.7 copy-start.6

commit v5 on v4

--- a/solution.py
+++ b/solution.py
@@ -36,7 +36,21 @@
     return lax.broadcasted_iota(I32, shape, dim)
 
 
-def plan_kernel(l0, l1, l2, l3, k0, k1, k2, k3, rows_flat, kinds_flat, req_out, meta, rows_out, kinds_out):
+def plan_kernel(
+    l0, k0, l1_any, l2_any, l3_any, k1_any, k2_any, k3_any,
+    rows_flat, kinds_flat, req_out, meta,
+    rows_out, kinds_out, l1, l2, l3, k1, k2, k3, in_s,
+):
+    loads = [
+        pltpu.make_async_copy(src, dst, in_s.at[i])
+        for i, (src, dst) in enumerate(
+            ((l1_any, l1), (l2_any, l2), (l3_any, l3), (k1_any, k1), (k2_any, k2), (k3_any, k3))
+        )
+    ]
+    for load in loads:
+        load.start()
+    for load in loads:
+        load.wait()
     me = lax.axis_index("boxes") * 4 + lax.axis_index("grp")
     rows_out[...] = jnp.full(rows_out.shape, ZERO_ROW, I32)
     kinds_out[...] = jnp.zeros(kinds_out.shape, I32)
@@ -116,12 +130,14 @@
             jax.ShapeDtypeStruct((SLOTS, 1, 128), I32),
             jax.ShapeDtypeStruct((8, 256), I32),
         ),
-        in_specs=[VMEM] * 8,
+        in_specs=[VMEM] * 2 + [ANY] * 6,
         out_specs=[VMEM] * 4,
-        scratch_shapes=[pltpu.VMEM((TARGETS, SLOT_PAD), I32)] * 2,
-        compiler_params=pltpu.CompilerParams(vmem_limit_bytes=32 << 20),
+        scratch_shapes=[pltpu.VMEM((TARGETS, SLOT_PAD), I32)] * 2
+        + [pltpu.VMEM((n, 189), I32) for n in (16, 2, 1)] * 2
+        + [pltpu.SemaphoreType.DMA((6,))],
+        compiler_params=pltpu.CompilerParams(vmem_limit_bytes=60 << 20),
         name="plan",
-    )(*lists, *kinds)
+    )(lists[0], kinds[0], *lists[1:], *kinds[1:])
 
 
 def left_half():
@@ -143,29 +159,38 @@
     )
 
 
-def weave(split):
+def weave(splits):
     lane = iota((32, 128), 1) & 63
     total = None
     for h in range(2):
         put = jnp.where(lane == 2 * iota((32, 128), 0) + h, 1.0, 0.0).astype(BF)
-        part = jnp.dot(split[h * 16 : (h + 1) * 16], put, preferred_element_type=F32)
+        rows = jnp.concatenate([x[h * 16 : (h + 1) * 16] for x in splits], axis=0)
+        part = jnp.dot(rows, put, preferred_element_type=F32)
         total = part if total is None else total + part
     return total.astype(BF)
 
 
-def unweave(block):
+def unweave(blocks):
+    x = jnp.concatenate(blocks, axis=0)
     parts = []
     for h in range(2):
-        row, lane = iota((128, 32), 0), iota((128, 32), 1)
-        put = jnp.where(row == 2 * lane + h, 1.0, 0.0).astype(BF)
-        parts.append(jnp.dot(block, put, preferred_element_type=F32))
-    return jnp.concatenate(parts, axis=0).astype(BF)
-
-
-def lowered(parent, matrix, local):
-    o = jnp.dot(parent, matrix, preferred_element_type=F32)
-    u = jnp.where(left_half(), o[0:16], o[16:32])
-    return (local + (u + pltpu.roll(u, 64, 1))).astype(BF)
+        put = jnp.where(iota((128, 32), 0) == 2 * iota((128, 32), 1) + h, 1.0, 0.0).astype(BF)
+        parts.append(jnp.dot(x, put, preferred_element_type=F32))
+    return [
+        jnp.concatenate([p[i * 16 : (i + 1) * 16] for p in parts], axis=0).astype(BF)
+        for i in range(len(blocks))
+    ]
+
+
+def lowered(parent, matrices, locals_):
+    left = left_half()
+    o = jnp.dot(parent, jnp.concatenate(matrices, axis=1), preferred_element_type=F32)
+    fields = []
+    for i, local in enumerate(locals_):
+        e = o[:, i * 128 : (i + 1) * 128]
+        u = jnp.where(left, e[0:16], e[16:32])
+        fields.append((local + (u + pltpu.roll(u, 64, 1))).astype(BF))
+    return fields
 
 
 def turn(coupling, weights, first, last, per):
@@ -177,10 +202,11 @@
     ]
     left = iota((32, 128), 1) < 64
 
-    def group(i):
+    def step(i, c):
+        base = (first + i * per) * 4
         rows = [[], []]
-        for j in range(2):
-            pair = coupling[pl.ds(i * 4 + 2 * j, 2)].reshape(256, 128)
+        for j in range(2 * per):
+            pair = coupling[pl.ds(base + 2 * j, 2)].reshape(256, 128)
             t = lax.dot_general(eye, pair, NT, preferred_element_type=F32).astype(BF)
             for k in range(2):
                 y = t[:, k * 128 : (k + 1) * 128]
@@ -192,16 +218,12 @@
             jnp.dot(jnp.concatenate(rows[h], axis=0), pick[h], preferred_element_type=F32).astype(BF)
             for h in range(2)
         ]
-        for k in range(4):
+        for k in range(4 * per):
             for p in range(2):
                 a = half[0][k * 32 : k * 32 + 32, p * 128 : (p + 1) * 128]
                 b = half[1][k * 32 : k * 32 + 32, p * 128 : (p + 1) * 128]
-                weights[i * 4 + k, 2 * p] = jnp.where(left, a, b)
-                weights[i * 4 + k, 2 * p + 1] = jnp.where(left, b, a)
-
-    def step(i, c):
-        for k in range(per):
-            group(first + i * per + k)
+                weights[base + k, 2 * p] = jnp.where(left, a, b)
+                weights[base + k, 2 * p + 1] = jnp.where(left, b, a)
         return c
 
     lax.fori_loop(0, (last - first) // per, step, 0)
@@ -219,7 +241,7 @@
     req, charges_any, basis_any, transfer, coupling_any,
     leaf_out, mu_out, coarse_out, own_leaf, weights_any,
     asked_v, asked_s, send, zbuf, coupling, weights, in_s, out_s,
-    charges, basis, leaf, mid, part,
+    charges, basis, leaf, split, mid, part,
     req_ss, req_rs, loc_s, leaf_ss, leaf_rs, mu_ss, mu_rs, z_ss, z_rs, y_ss, y_rs, x_ss, x_rs,
 ):
     box = lax.axis_index("boxes")
@@ -305,19 +327,27 @@
     loads[1].wait()
 
     def boxes(i, c):
-        blocks = []
-        for k in range(8):
-            b = i * 8 + k
-            w = basis[b]
-            points = charges[:, pl.ds(pl.multiple_of(b * 256, 256), 256)]
-            m = lax.dot_general(
-                points, jnp.concatenate([w, w], axis=0), NT, preferred_element_type=F32
-            ).astype(BF)
-            leaf[b] = m
-            blocks.append(m)
-        for k in range(4):
-            place = pl.ds(pl.multiple_of((i * 4 + k) * 16, 16), 16)
-            own_leaf[place, :] = jnp.where(left, blocks[2 * k], blocks[2 * k + 1])
+        for q in range(2):
+            b = i * 8 + q * 4
+            points = [
+                charges[:, pl.ds(pl.multiple_of((b + j) * 256, 256), 256)] for j in range(4)
+            ]
+            o = lax.dot_general(
+                jnp.concatenate(points, axis=0),
+                basis[pl.ds(b, 4)].reshape(256, 256),
+                NT,
+                preferred_element_type=F32,
+            )
+            for h in range(2):
+                lanes = slice(h * 128, (h + 1) * 128)
+                pair = jnp.where(
+                    left, o[h * 32 : h * 32 + 16, lanes], o[h * 32 + 16 : h * 32 + 32, lanes]
+                )
+                turned = pltpu.roll(pair, 64, 1)
+                leaf[b + 2 * h] = jnp.where(left, pair, turned).astype(BF)
+                leaf[b + 2 * h + 1] = jnp.where(left, turned, pair).astype(BF)
+                place = pl.ds(pl.multiple_of((i * 4 + q * 2 + h) * 16, 16), 16)
+                own_leaf[place, :] = pair.astype(BF)
         return c
 
     lax.fori_loop(0, LEAFS // 8, boxes, 0)
@@ -351,20 +381,22 @@
     def mids(i, c):
         for k in range(4):
             t = i * 4 + k
-            mid[t] = weave(
-                lift([leaf[t * 8 + j] for j in range(8)], [transfer[t * 8 + j] for j in range(8)])
-                .astype(BF)
-            )
+            split[t] = lift(
+                [leaf[t * 8 + j] for j in range(8)], [transfer[t * 8 + j] for j in range(8)]
+            ).astype(BF)
         return c
 
     lax.fori_loop(0, 4, mids, 0)
+    mid[...] = weave([split[t] for t in range(16)]).reshape(16, 16, 128)
     for q in range(8):
         mu_out[REACH, q * 16 : (q + 1) * 16, :] = jnp.where(left, mid[2 * q], mid[2 * q + 1])
     upper = []
     for t in range(2):
         children = range(t * 8, t * 8 + 8)
         sums = lift([mid[j] for j in children], [transfer[128 + j] for j in children])
-        upper.append(weave(sums.astype(BF)))
+        upper.append(sums.astype(BF))
+    upper = weave(upper)
+    upper = [upper[0:16], upper[16:32]]
     mu_out[REACH, 128:144, :] = jnp.where(left, upper[0], upper[1])
     part[...] = jnp.zeros(part.shape, F32)
     part[:, 0:32] = lift(upper, [transfer[144], transfer[145]])
@@ -375,7 +407,7 @@
     turn_part(0)
     each(3, 1, lambda i: z_copy(i).wait())
     whole = (zbuf[0] + zbuf[1] + zbuf[2] + zbuf[3]).astype(BF)
-    coarse_out[box] = weave(whole[:, 0:32])
+    coarse_out[box] = weave([whole[:, 0:32]])
     each(7, 1, lambda i: y_copy(i).start())
     turn_part(1)
     each(7, 1, lambda i: y_copy(i).wait())
@@ -415,27 +447,32 @@
             pltpu.VMEM((16, 32768), BF),
             pltpu.VMEM((LEAFS, 64, 256), BF),
             pltpu.VMEM((LEAFS, 16, 128), BF),
+            pltpu.VMEM((16, 32, 32), BF),
             pltpu.VMEM((16, 16, 128), BF),
             pltpu.VMEM((32, 128), F32),
         ]
         + [sem((SLOTS,))] * 7
         + [sem((8,))] * 6,
         compiler_params=pltpu.CompilerParams(
-            collective_id=0, has_side_effects=True, vmem_limit_bytes=50 << 20
+            collective_id=0, has_side_effects=True, vmem_limit_bytes=60 << 20
         ),
         name="exchange",
     )(req, charges, basis, transfer, coupling)
 
 
 def far_kernel(
-    rows_idx, kinds_idx, req, meta, own_leaf, leaf_in, mu_in, coarse_in, transfer,
-    weights_any, basis_any, out,
-    table, weights, basis, local, parents, in_s,
+    req, meta, own_leaf, leaf_in, mu_in, coarse_in, transfer,
+    rows_any, kinds_any, weights_any, basis_any, out,
+    rows_idx, kinds_idx, table, weights, basis, local, parents, in_s,
 ):
-    load = pltpu.make_async_copy(weights_any, weights, in_s.at[0])
-    load_basis = pltpu.make_async_copy(basis_any, basis, in_s.at[1])
-    load.start()
-    load_basis.start()
+    loads = [
+        pltpu.make_async_copy(rows_any, rows_idx, in_s.at[0]),
+        pltpu.make_async_copy(kinds_any, kinds_idx, in_s.at[1]),
+        pltpu.make_async_copy(weights_any, weights, in_s.at[2]),
+    ]
+    load_basis = pltpu.make_async_copy(basis_any, basis, in_s.at[3])
+    for load in loads:
+        load.start()
     l = iota((128, 512), 0)
     n = iota((128, 512), 1)
     spread = jnp.where(l == (n >> 7) * 32 + (n & 31), 1.0, 0.0).astype(BF)
@@ -493,7 +530,9 @@
 
     lax.fori_loop(0, 4, coarse, 0)
 
-    load.wait()
+    for load in loads:
+        load.wait()
+    load_basis.start()
     lane = iota((32, 128), 1)
     m1, m2, m3 = lane < 32, lane < 64, lane < 96
     left = iota((16, 128), 1) < 64
@@ -542,42 +581,71 @@
         first = last
 
     load_basis.wait()
-    coarse_field = unweave(local[146].astype(BF))
+    (coarse_field,) = unweave([local[146].astype(BF)])
+    upper_fields = unweave(
+        lowered(coarse_field, [transfer[144], transfer[145]], [local[144], local[145]])
+    )
+    mid_fields = []
     for u in range(2):
-        upper_field = unweave(lowered(coarse_field, transfer[144 + u], local[144 + u]))
-        for m in range(u * 8, u * 8 + 8):
-            parents[m] = unweave(lowered(upper_field, transfer[128 + m], local[128 + m]))
-
-    def boxes(m, c):
-        parent = parents[m]
-        for j in range(8):
-            b = m * 8 + j
-            field = lowered(parent, transfer[b], local[b])
-            points = jnp.dot(field[:, :64], basis[b], preferred_element_type=F32)
-            out[:, pl.ds(pl.multiple_of(b * 256, 256), 256)] = points.astype(BF)
-        return c
-
-    lax.fori_loop(0, 16, boxes, 0)
+        children = range(u * 8, u * 8 + 8)
+        mid_fields += lowered(
+            upper_fields[u], [transfer[128 + m] for m in children], [local[128 + m] for m in children]
+        )
+    for m, field in enumerate(unweave(mid_fields)):
+        parents[m] = field
+
+    zero = jnp.zeros((16, 128), BF)
+
+    def boxes(m):
+        fields = lowered(
+            parents[m],
+            [transfer[m * 8 + j] for j in range(8)],
+            [local[m * 8 + j] for j in range(8)],
+        )
+        for q in range(2):
+            rows = []
+            for j in range(4):
+                f = fields[q * 4 + j]
+                f = jnp.where(left, zero, f) if j % 2 else jnp.where(left, f, zero)
+                rows.append(jnp.concatenate([zero, f] if j > 1 else [f, zero], axis=1))
+            b = m * 8 + q * 4
+            points = jnp.dot(
+                jnp.concatenate(rows, axis=0),
+                basis[pl.ds(b, 4)].reshape(256, 256),
+                preferred_element_type=F32,
+            ).astype(BF)
+            for j in range(4):
+                place = pl.ds(pl.multiple_of((b + j) * 256, 256), 256)
+                out[:, place] = points[j * 16 : (j + 1) * 16]
+
+    def two(i, c):
+        boxes(2 * i)
+        boxes(2 * i + 1)
+        return c
+
+    lax.fori_loop(0, 8, two, 0)
 
 
 def far(rows_idx, kinds_idx, req, meta, own_leaf, leaf_in, mu_in, coarse_in, transfer, weights, basis):
     return pl.pallas_call(
         far_kernel,
         out_shape=jax.ShapeDtypeStruct((16, LEAFS * 256), BF),
-        in_specs=[SMEM] * 4 + [VMEM] * 5 + [ANY] * 2,
+        in_specs=[SMEM] * 2 + [VMEM] * 5 + [ANY] * 4,
         out_specs=VMEM,
         scratch_shapes=[
+            pltpu.SMEM((TARGETS * 256,), I32),
+            pltpu.SMEM((TARGETS * 256,), I32),
             pltpu.VMEM((TABLE_ROWS, 32, 128), BF),
             pltpu.VMEM((4 * KINDS, 32, 128), BF),
             pltpu.VMEM((LEAFS, 64, 256), BF),
             pltpu.VMEM((TARGETS, 16, 128), F32),
             pltpu.VMEM((16, 32, 32), BF),
-            pltpu.SemaphoreType.DMA((2,)),
+            pltpu.SemaphoreType.DMA((4,)),
         ],
         compiler_params=pltpu.CompilerParams(vmem_limit_bytes=60 << 20),
         name="far",
     )(
-        rows_idx, kinds_idx, req, meta, own_leaf, leaf_in, mu_in, coarse_in, transfer, weights, basis
+        req, meta, own_leaf, leaf_in, mu_in, coarse_in, transfer, rows_idx, kinds_idx, weights, basis
     )
 
 

time: 172 us -> 149 us (0.87)
  Pallas kernels: 161 us -> 141 us
  local copies, waits for them, and re-layouts: 9.61 us -> 4.81 us
    pallas_call x1, Pallas kernels: 86.7 us -> 69.7 us  [far(): pl.pallas_call(far_kernel, out_shape=jax.ShapeDtypeStruct((16, LEAFS * 25...]
    unnamed x33 -> x3, local copies, waits for them, and re-layouts: 9.41 us -> 3.52 us
    pallas_call x1, Pallas kernels: 66.5 us -> 61.8 us  [exchange(): pl.pallas_call(exchange_kernel, out_shape=(jax.ShapeDtypeStruct((SLOTS, 2...]
    pallas_call x1, Pallas kernels: 7.32 us -> 9.72 us  [plan(): pl.pallas_call(plan_kernel, out_shape=(jax.ShapeDtypeStruct((2 * TARGETS,...]
where the time goes in v5:
time: 149 us; the launch traced here: 148 us
  Pallas kernels  141 us (95%)
  local copies, waits for them, and re-layouts  4.81 us (3%)
    pallas_call x1, Pallas kernels, far(): pl.pallas_call(far_kernel, out_shape=jax.ShapeDtypeStruct((16, LEAFS * 25...  69.7 us
    pallas_call x1, Pallas kernels, exchange(): pl.pallas_call(exchange_kernel, out_shape=(jax.ShapeDtypeStruct((SLOTS, 2...  61.8 us
    pallas_call x1, Pallas kernels, plan(): pl.pallas_call(plan_kernel, out_shape=(jax.ShapeDtypeStruct((2 * TARGETS,...  9.72 us
    unnamed x3, local copies, waits for them, and re-layouts  3.52 us

profile of v5, /device:TPU:25, one launch (start us, length us, event | category | flops | bytes accessed | tf_op | source)
XLA Modules:
  0.0 147.6 jit_solution(16102403516358396987)
XLA Ops:
  0.0 1.6 %copy.15.l0 = s32[128,189]{1,0:T(8,128)} copy(s32[128,189]{0,1:T(8,128)} %param.20) | data formatting | bytes 193536 | tf_op args[6]
  1.6 1.6 %copy.16.k0 = s32[128,189]{1,0:T(8,128)} copy(s32[128,189]{0,1:T(8,128)} %param.24) | data formatting | bytes 193536 | tf_op args[10]
  3.3 9.7 %plan.1 = (s32[296,128]{1,0:T(8,128)}, s32[296,128]{1,0:T(8,128)}, s32[28,1,128]{2,1,0:T(1,128)}, s32[8,256]{1,0:T(8,128)}) custom-call(s32[128,189]{1,0:T(8,128)} %copy.15.l0, s32[128,189]{1,0:T(8,128)} %copy.16.k0, s32[16,189]{1,0:T(8,128)} %l1_any.1, s32[2,189]{1,0:T(2,128)} %l2_any.1, s32[1,189]{1,0:T(1,128)} %l3_any.1, s32[16,189]{1,0:T(8,128)} %k1_any.1, ...), custom_call_target="tpu_custom_call" | custom-call | tf_op jit(solution)/shard_map/plan/pallas_call | solution.py:125
  13.0 1.4 pad_maximum_fusion
  14.4 0.2 copy.18
  14.7 1.3 slice.transfer
  16.0 61.8 %exchange.1 = (bf16[28,256,128]{2,1,0:T(8,128)(2,1)}, bf16[28,144,128]{2,1,0:T(8,128)(2,1)}, bf16[32,16,128]{2,1,0:T(8,128)(2,1)}, bf16[1024,128]{1,0:T(8,128)(2,1)}, bf16[316,4,32,128]{3,2,1,0:T(8,128)(2,1)}) custom-call(s32[28,1,128]{2,1,0:T(1,128)} %get-tuple-element.14.req, bf16[16,32768]{1,0:T(8,128)(2,1)} %charges_any.1, ...), custom_call_target="tpu_custom_call" | custom-call | tf_op jit(solution)/shard_map/exchange/pallas_call | solution.py:427
  77.8 69.7 %far.1 = bf16[16,32768]{1,0:T(8,128)(2,1)} custom-call(s32[28,1,128]{2,1,0:T(1,128)} %get-tuple-element.14.req, s32[8,256]{1,0:T(8,128)} %get-tuple-element.15.meta, bf16[1024,128]{1,0:T(8,128)(2,1)} %get-tuple-element.16.own_leaf, bf16[28,256,128]{2,1,0:T(8,128)(2,1)} %get-tuple-element.17.leaf_in, bf16[28,144,128]{2,1,0:T(8,128)(2,1)} %get-tuple-element.18.mu_in, ...), custom_call_target="tpu_custom_call" | custom-call | tf_op jit(solution)/shard_map/far/pallas_call | solution.py:630

commit v6 on v5

--- a/solution.py
+++ b/solution.py
@@ -37,9 +37,9 @@
 
 
 def plan_kernel(
-    l0, k0, l1_any, l2_any, l3_any, k1_any, k2_any, k3_any,
+    l0_across, k0_across, l1_any, l2_any, l3_any, k1_any, k2_any, k3_any,
     rows_flat, kinds_flat, req_out, meta,
-    rows_out, kinds_out, l1, l2, l3, k1, k2, k3, in_s,
+    rows_out, kinds_out, l0, k0, pad, l1, l2, l3, k1, k2, k3, in_s,
 ):
     loads = [
         pltpu.make_async_copy(src, dst, in_s.at[i])
@@ -49,6 +49,10 @@
     ]
     for load in loads:
         load.start()
+    pad[...] = jnp.zeros(pad.shape, I32)
+    for across, tiled in ((l0_across, l0), (k0_across, k0)):
+        pad[0:189, :] = across[...]
+        tiled[...] = pad[...].T
     for load in loads:
         load.wait()
     me = lax.axis_index("boxes") * 4 + lax.axis_index("grp")
@@ -58,13 +62,13 @@
     for level, (lists, kinds, count, offset) in enumerate(
         ((l0, k0, 128, 0), (l1, k1, 16, MID_ROW), (l2, k2, 2, UPPER_ROW))
     ):
-        ids = lists[...]
+        ids = lists[...][:, 0:189]
         whole = DEV * count
         rel = lax.rem(ids - (me - REACH) * count + whole, whole)
         far = (REACH + DEV // 2) * count
         rel = jnp.where(rel >= far, rel - far + (SLOTS - 1) * count, rel)
         rows_out[start : start + count, 0:189] = jnp.where(ids >= 0, rel + offset, ZERO_ROW)
-        kinds_out[start : start + count, 0:189] = kinds[...] * 4 + level
+        kinds_out[start : start + count, 0:189] = kinds[...][:, 0:189] * 4 + level
         start += count
     ids = l3[...]
     rows_out[start : start + 1, 0:189] = jnp.where(ids >= 0, ids + COARSE_ROW, ZERO_ROW)
@@ -93,13 +97,18 @@
     sub_lo = iota((LEAFS, SLOT_PAD), 0)
     sub_hi = iota((32, SLOT_PAD), 0)
 
-    def mark(t, seen):
-        row = rows_out[pl.ds(t, 1), :]
-        lo = jnp.where(sub_lo == (row & 127), 1.0, 0.0).astype(BF)
-        hi = jnp.where(sub_hi == (row >> 7), 1.0, 0.0).astype(BF)
-        return seen + lax.dot_general(hi, lo, NT, preferred_element_type=F32)
-
-    seen = lax.fori_loop(0, LEAFS, mark, jnp.zeros((32, LEAFS), F32), unroll=4)
+    def mark(i, seen):
+        lo, hi = [], []
+        for k in range(2):
+            row = rows_out[pl.ds(2 * i + k, 1), :]
+            lo.append(jnp.where(sub_lo == (row & 127), 1.0, 0.0).astype(BF))
+            hi.append(jnp.where(sub_hi == (row >> 7), 1.0, 0.0).astype(BF))
+        return seen + lax.dot_general(
+            jnp.concatenate(hi, axis=0), jnp.concatenate(lo, axis=0), NT, preferred_element_type=F32
+        )
+
+    seen = lax.fori_loop(0, LEAFS // 2, mark, jnp.zeros((64, 2 * LEAFS), F32), unroll=4)
+    seen = seen[0:32, 0:LEAFS] + seen[32:64, LEAFS:]
     needed = seen > 0.5
     lane = iota((32, LEAFS), 1)
     upto = (
@@ -133,11 +142,13 @@
         in_specs=[VMEM] * 2 + [ANY] * 6,
         out_specs=[VMEM] * 4,
         scratch_shapes=[pltpu.VMEM((TARGETS, SLOT_PAD), I32)] * 2
+        + [pltpu.VMEM((LEAFS, 256), I32)] * 2
+        + [pltpu.VMEM((256, LEAFS), I32)]
         + [pltpu.VMEM((n, 189), I32) for n in (16, 2, 1)] * 2
         + [pltpu.SemaphoreType.DMA((6,))],
         compiler_params=pltpu.CompilerParams(vmem_limit_bytes=60 << 20),
         name="plan",
-    )(lists[0], kinds[0], *lists[1:], *kinds[1:])
+    )(lists[0].T, kinds[0].T, *lists[1:], *kinds[1:])
 
 
 def left_half():
@@ -362,22 +373,6 @@
         span = pl.ds(TURN_PARTS[k][0] * 4, (TURN_PARTS[k][1] - TURN_PARTS[k][0]) * 4)
         return pltpu.make_async_copy(weights.at[span], weights_any.at[span], out_s.at[k])
 
-    asked_v[REACH] = jnp.zeros((1, 128), I32)
-    each(SLOTS - 1, 0, lambda i: req_copy(slot_of(i)).wait_recv())
-    local = pltpu.make_async_copy(asked_v, asked_s, loc_s.at[0])
-    local.start()
-    local.wait()
-
-    def serve(i):
-        p = slot_of(i)
-        for q in range(ROOM // 2):
-            a = leaf[asked_s[p, 0, 2 * q]]
-            b = leaf[asked_s[p, 0, 2 * q + 1]]
-            send[p, q * 16 : (q + 1) * 16, :] = jnp.where(left, a, b)
-        leaf_copy(p).start()
-
-    each(SLOTS - 1, 0, serve)
-
     def mids(i, c):
         for k in range(4):
             t = i * 4 + k
@@ -403,6 +398,22 @@
     zbuf[grp] = part[...]
     each(3, 1, lambda i: z_copy(i).start())
     each(SLOTS - 1, 0, lambda i: mu_copy(slot_of(i)).start())
+    asked_v[REACH] = jnp.zeros((1, 128), I32)
+    each(SLOTS - 1, 0, lambda i: req_copy(slot_of(i)).wait_recv())
+    local = pltpu.make_async_copy(asked_v, asked_s, loc_s.at[0])
+    local.start()
+    local.wait()
+
+    def serve(i):
+        p = slot_of(i)
+        for q in range(ROOM // 2):
+            a = leaf[asked_s[p, 0, 2 * q]]
+            b = leaf[asked_s[p, 0, 2 * q + 1]]
+            send[p, q * 16 : (q + 1) * 16, :] = jnp.where(left, a, b)
+        leaf_copy(p).start()
+
+    each(SLOTS - 1, 0, serve)
+
     loads[2].wait()
     turn_part(0)
     each(3, 1, lambda i: z_copy(i).wait())

time: 149 us -> 144 us (0.966)
  local copies, waits for them, and re-layouts: 4.81 us -> 1.54 us
    unnamed x3 -> x1, local copies, waits for them, and re-layouts: 3.52 us -> 0.25 us
    pallas_call x1, Pallas kernels: 9.72 us -> 7.67 us  [plan(): pl.pallas_call(plan_kernel, out_shape=(jax.ShapeDtypeStruct((2 * TARGETS,...]
where the time goes in v6:
time: 144 us
  Pallas kernels  141 us (98%)
  local copies, waits for them, and re-layouts  1.54 us (1%)
    pallas_call x1, Pallas kernels, far(): pl.pallas_call(far_kernel, out_shape=jax.ShapeDtypeStruct((16, LEAFS * 25...  70.5 us
    pallas_call x1, Pallas kernels, exchange(): pl.pallas_call(exchange_kernel, out_shape=(jax.ShapeDtypeStruct((SLOTS, 2...  62.4 us
    pallas_call x1, Pallas kernels, plan(): pl.pallas_call(plan_kernel, out_shape=(jax.ShapeDtypeStruct((2 * TARGETS,...  7.67 us

profile of v6, /device:TPU:25, one launch (start us, length us, event | category | flops | bytes accessed | tf_op | source)
XLA Modules:
  0.0 143.7 jit_solution(2918637371679063631)
XLA Ops:
  0.0 7.7 %plan.1 = (s32[296,128]{1,0:T(8,128)}, s32[296,128]{1,0:T(8,128)}, s32[28,1,128]{2,1,0:T(1,128)}, s32[8,256]{1,0:T(8,128)}) custom-call(s32[189,128]{1,0:T(8,128)} %bitcast.21, s32[189,128]{1,0:T(8,128)} %bitcast.22, s32[16,189]{1,0:T(8,128)} %l1_any.1, s32[2,189]{1,0:T(2,128)} %l2_any.1, s32[1,189]{1,0:T(1,128)} %l3_any.1, s32[16,189]{1,0:T(8,128)} %k1_any.1, ...), custom_call_target="tpu_custom_call" | custom-call | tf_op jit(solution)/shard_map/plan/pallas_call | solution.py:134
  7.7 1.4 pad_maximum_fusion
  9.1 0.2 copy.16
  9.4 1.3 slice.transfer
  10.7 62.4 %exchange.1 = (bf16[28,256,128]{2,1,0:T(8,128)(2,1)}, bf16[28,144,128]{2,1,0:T(8,128)(2,1)}, bf16[32,16,128]{2,1,0:T(8,128)(2,1)}, bf16[1024,128]{1,0:T(8,128)(2,1)}, bf16[316,4,32,128]{3,2,1,0:T(8,128)(2,1)}) custom-call(s32[28,1,128]{2,1,0:T(1,128)} %get-tuple-element.14.req, bf16[16,32768]{1,0:T(8,128)(2,1)} %charges_any.1, ...), custom_call_target="tpu_custom_call" | custom-call | tf_op jit(solution)/shard_map/exchange/pallas_call | solution.py:438
  73.0 70.5 %far.1 = bf16[16,32768]{1,0:T(8,128)(2,1)} custom-call(s32[28,1,128]{2,1,0:T(1,128)} %get-tuple-element.14.req, s32[8,256]{1,0:T(8,128)} %get-tuple-element.15.meta, bf16[1024,128]{1,0:T(8,128)(2,1)} %get-tuple-element.16.own_leaf, bf16[28,256,128]{2,1,0:T(8,128)(2,1)} %get-tuple-element.17.leaf_in, bf16[28,144,128]{2,1,0:T(8,128)(2,1)} %get-tuple-element.18.mu_in, ...), custom_call_target="tpu_custom_call" | custom-call | tf_op jit(solution)/shard_map/far/pallas_call | solution.py:641

commit v7 on v6

--- a/solution.py
+++ b/solution.py
@@ -249,10 +249,10 @@
 
 
 def exchange_kernel(
-    req, charges_any, basis_any, transfer, coupling_any,
+    req, charges_any, basis_any, transfer_any, coupling_any,
     leaf_out, mu_out, coarse_out, own_leaf, weights_any,
     asked_v, asked_s, send, zbuf, coupling, weights, in_s, out_s,
-    charges, basis, leaf, split, mid, part,
+    charges, basis, leaf, split, mid, part, transfer,
     req_ss, req_rs, loc_s, leaf_ss, leaf_rs, mu_ss, mu_rs, z_ss, z_rs, y_ss, y_rs, x_ss, x_rs,
 ):
     box = lax.axis_index("boxes")
@@ -282,6 +282,7 @@
         pltpu.make_async_copy(charges_any, charges, in_s.at[0]),
         pltpu.make_async_copy(basis_any, basis, in_s.at[1]),
         pltpu.make_async_copy(coupling_any, coupling, in_s.at[2]),
+        pltpu.make_async_copy(transfer_any, transfer, in_s.at[3]),
     ]
     for load in loads:
         load.start()
@@ -373,6 +374,8 @@
         span = pl.ds(TURN_PARTS[k][0] * 4, (TURN_PARTS[k][1] - TURN_PARTS[k][0]) * 4)
         return pltpu.make_async_copy(weights.at[span], weights_any.at[span], out_s.at[k])
 
+    loads[3].wait()
+
     def mids(i, c):
         for k in range(4):
             t = i * 4 + k
@@ -444,7 +447,7 @@
             jax.ShapeDtypeStruct((1024, 128), BF),
             jax.ShapeDtypeStruct((KINDS, 4, 32, 128), BF),
         ),
-        in_specs=[VMEM, ANY, ANY, VMEM, ANY],
+        in_specs=[VMEM] + [ANY] * 4,
         out_specs=[VMEM] * 4 + [ANY],
         scratch_shapes=[
             pltpu.VMEM((SLOTS, 1, 128), I32),
@@ -453,7 +456,7 @@
             pltpu.VMEM((4, 32, 128), F32),
             pltpu.VMEM((KINDS, 128, 128), BF),
             pltpu.VMEM((KINDS, 4, 32, 128), BF),
-            sem((3,)),
+            sem((4,)),
             sem((len(TURN_PARTS),)),
             pltpu.VMEM((16, 32768), BF),
             pltpu.VMEM((LEAFS, 64, 256), BF),
@@ -461,6 +464,7 @@
             pltpu.VMEM((16, 32, 32), BF),
             pltpu.VMEM((16, 16, 128), BF),
             pltpu.VMEM((32, 128), F32),
+            pltpu.VMEM((146, 32, 128), BF),
         ]
         + [sem((SLOTS,))] * 7
         + [sem((8,))] * 6,
@@ -472,9 +476,9 @@
 
 
 def far_kernel(
-    req, meta, own_leaf, leaf_in, mu_in, coarse_in, transfer,
-    rows_any, kinds_any, weights_any, basis_any, out,
-    rows_idx, kinds_idx, table, weights, basis, local, parents, in_s,
+    req, meta, own_leaf, leaf_in, mu_in, coarse_in,
+    rows_any, kinds_any, weights_any, basis_any, transfer_any, out,
+    rows_idx, kinds_idx, table, weights, basis, transfer, local, parents, in_s,
 ):
     loads = [
         pltpu.make_async_copy(rows_any, rows_idx, in_s.at[0]),
@@ -482,6 +486,7 @@
         pltpu.make_async_copy(weights_any, weights, in_s.at[2]),
     ]
     load_basis = pltpu.make_async_copy(basis_any, basis, in_s.at[3])
+    load_transfer = pltpu.make_async_copy(transfer_any, transfer, in_s.at[4])
     for load in loads:
         load.start()
     l = iota((128, 512), 0)
@@ -544,6 +549,7 @@
     for load in loads:
         load.wait()
     load_basis.start()
+    load_transfer.start()
     lane = iota((32, 128), 1)
     m1, m2, m3 = lane < 32, lane < 64, lane < 96
     left = iota((16, 128), 1) < 64
@@ -592,6 +598,7 @@
         first = last
 
     load_basis.wait()
+    load_transfer.wait()
     (coarse_field,) = unweave([local[146].astype(BF)])
     upper_fields = unweave(
         lowered(coarse_field, [transfer[144], transfer[145]], [local[144], local[145]])
@@ -641,7 +648,7 @@
     return pl.pallas_call(
         far_kernel,
         out_shape=jax.ShapeDtypeStruct((16, LEAFS * 256), BF),
-        in_specs=[SMEM] * 2 + [VMEM] * 5 + [ANY] * 4,
+        in_specs=[SMEM] * 2 + [VMEM] * 4 + [ANY] * 5,
         out_specs=VMEM,
         scratch_shapes=[
             pltpu.SMEM((TARGETS * 256,), I32),
@@ -649,14 +656,15 @@
             pltpu.VMEM((TABLE_ROWS, 32, 128), BF),
             pltpu.VMEM((4 * KINDS, 32, 128), BF),
             pltpu.VMEM((LEAFS, 64, 256), BF),
+            pltpu.VMEM((146, 32, 128), BF),
             pltpu.VMEM((TARGETS, 16, 128), F32),
             pltpu.VMEM((16, 32, 32), BF),
-            pltpu.SemaphoreType.DMA((4,)),
+            pltpu.SemaphoreType.DMA((5,)),
         ],
         compiler_params=pltpu.CompilerParams(vmem_limit_bytes=60 << 20),
         name="far",
     )(
-        req, meta, own_leaf, leaf_in, mu_in, coarse_in, transfer, rows_idx, kinds_idx, weights, basis
+        req, meta, own_leaf, leaf_in, mu_in, coarse_in, rows_idx, kinds_idx, weights, basis, transfer
     )
 
 

time: 144 us -> 144 us (level); the launches traced: 144 us -> 141 us
  Pallas kernels: 141 us -> 138 us
    pallas_call x1, Pallas kernels: 70.5 us -> 68.5 us  [far(): pl.pallas_call(far_kernel, out_shape=jax.ShapeDtypeStruct((16, LEAFS * 25...]
where the time goes in v7:
time: 144 us; the launch traced here: 141 us
  Pallas kernels  138 us (96%)
  local copies, waits for them, and re-layouts  1.54 us (1%)
    pallas_call x1, Pallas kernels, far(): pl.pallas_call(far_kernel, out_shape=jax.ShapeDtypeStruct((16, LEAFS * 25...  68.5 us
    pallas_call x1, Pallas kernels, exchange(): pl.pallas_call(exchange_kernel, out_shape=(jax.ShapeDtypeStruct((SLOTS, 2...  61.7 us
    pallas_call x1, Pallas kernels, plan(): pl.pallas_call(plan_kernel, out_shape=(jax.ShapeDtypeStruct((2 * TARGETS,...  7.67 us

profile of v7, /device:TPU:25, one launch (start us, length us, event | category | flops | bytes accessed | tf_op | source)
XLA Modules:
  0.0 141.1 jit_solution(7659538174548922687)
XLA Ops:
  0.0 7.7 %plan.1 = (s32[296,128]{1,0:T(8,128)}, s32[296,128]{1,0:T(8,128)}, s32[28,1,128]{2,1,0:T(1,128)}, s32[8,256]{1,0:T(8,128)}) custom-call(s32[189,128]{1,0:T(8,128)} %bitcast.21, s32[189,128]{1,0:T(8,128)} %bitcast.22, s32[16,189]{1,0:T(8,128)} %l1_any.1, s32[2,189]{1,0:T(2,128)} %l2_any.1, s32[1,189]{1,0:T(1,128)} %l3_any.1, s32[16,189]{1,0:T(8,128)} %k1_any.1, ...), custom_call_target="tpu_custom_call" | custom-call | tf_op jit(solution)/shard_map/plan/pallas_call | solution.py:134
  7.7 1.4 %pad_maximum_fusion = bf16[146,4096]{1,0:T(8,128)(2,1)S(1)} fusion(bf16[2,4096]{1,0:T(2,128)(2,1)} %param.18, bf16[16,4096]{1,0:T(8,128)(2,1)} %param.17, bf16[128,4096]{1,0:T(8,128)(2,1)} %param.16), kind=kLoop, calls=%fused_computation | loop fusion | flops 3588096 | bytes 2392064 | tf_op jit(solution)/shard_map/concatenate | solution.py:675
  9.1 0.2 copy.16
  9.4 1.3 slice.transfer_any
  10.7 61.7 %exchange.1 = (bf16[28,256,128]{2,1,0:T(8,128)(2,1)}, bf16[28,144,128]{2,1,0:T(8,128)(2,1)}, bf16[32,16,128]{2,1,0:T(8,128)(2,1)}, bf16[1024,128]{1,0:T(8,128)(2,1)}, bf16[316,4,32,128]{3,2,1,0:T(8,128)(2,1)}) custom-call(s32[28,1,128]{2,1,0:T(1,128)} %get-tuple-element.14.req, bf16[16,32768]{1,0:T(8,128)(2,1)} %charges_any.1, ...), custom_call_target="tpu_custom_call" | custom-call | tf_op jit(solution)/shard_map/exchange/pallas_call | solution.py:441
  72.4 68.5 %far.1 = bf16[16,32768]{1,0:T(8,128)(2,1)} custom-call(s32[28,1,128]{2,1,0:T(1,128)} %get-tuple-element.14.req, s32[8,256]{1,0:T(8,128)} %get-tuple-element.15.meta, bf16[1024,128]{1,0:T(8,128)(2,1)} %get-tuple-element.16.own_leaf, bf16[28,256,128]{2,1,0:T(8,128)(2,1)} %get-tuple-element.17.leaf_in, bf16[28,144,128]{2,1,0:T(8,128)(2,1)} %get-tuple-element.18.mu_in, ...), custom_call_target="tpu_custom_call" | custom-call | tf_op jit(solution)/shard_map/far/pallas_call | solution.py:648
